TPU v7x, 256 devices: a whole 4x4x8 slice. The times are simulated.
256 devices in a mesh: gx: 16 (over x, y_lo, core), gy: 16 (over z, y_hi).
Axes of the slice: x: 4, y: 4 (y_hi: 2, y_lo: 2; y = y_hi * 2 + y_lo), z: 8, core: 2. Of those that a mesh axis runs over, the one named last changes fastest.
Arguments:
- tensor: float32 [16, 6144, 6144], P(None, 'gx', 'gy'), may hold values from -6 to 6
- factor_b_init: float32 [6144, 128], P(('gy', 'gx')), may hold values from 0 to 1
- time_init: float32 [16, 128], replicated, may hold values from 0 to 1
Outputs:
- factor_a: float32 [6144, 128], P(('gx', 'gy'))
- factor_b: float32 [6144, 128], P(('gy', 'gx'))
- time_factor: float32 [16, 128], replicated
All inputs are finite; a program needn't handle non-finite values.
Results may differ from a plain program's by a relative error of at most 0.00029.
Values sent between devices are 32-bit elements; how exact they have to be, the bound alone decides.
No kernel may reach another device: no remote copies, remote signals or barrier semaphores. Data moves between devices by JAX's collectives and lax.ppermute only.
A program may use at most 64 MiB of HBM per device.

v0:
```python
import jax
import jax.numpy as jnp
from jax import lax
from jax.sharding import PartitionSpec as P

highest = lax.Precision.HIGHEST
epsilon = 1e-06


def solve_rows(metric, rhs):
    lower = jnp.linalg.cholesky(metric)
    return jax.scipy.linalg.cho_solve((lower, True), rhs.T).T


def gram_of(matrix):
    return lax.dot_general(matrix, matrix, (((0,), (0,)), ((), ())), precision=highest)


def scaled(gram_raw):
    norms = jnp.sqrt(jnp.diagonal(gram_raw) + epsilon)
    return (norms, gram_raw / (norms[:, None] * norms[None, :]))


def shards(tensor, factor_b_init, time_init):
    devices_x = lax.axis_size("gx")
    devices_y = lax.axis_size("gy")
    rows_first = tensor.shape[1]
    rows_second = tensor.shape[2]
    gram_time = gram_of(time_init)
    gram_old = lax.psum(gram_of(factor_b_init), ("gx", "gy"))
    block_old = lax.all_gather(factor_b_init, "gx", axis=0, tiled=True)
    along_j = lax.dot_general(tensor, block_old, (((2,), (0,)), ((), ())), precision=highest)
    partial_a = jnp.einsum("kir,kr->ir", along_j, time_init, precision=highest)
    metric_a = gram_old * gram_time
    summed_a = lax.psum_scatter(partial_a, "gy", scatter_dimension=0, tiled=True)
    raw_a = solve_rows(metric_a, summed_a)
    gram_raw_a = lax.psum(gram_of(raw_a), ("gx", "gy"))
    norm_a, gram_a = scaled(gram_raw_a)
    mine_a = raw_a / norm_a
    block_a = lax.all_gather(mine_a, "gy", axis=0, tiled=True)
    along_i = lax.dot_general(tensor, block_a, (((1,), (0,)), ((), ())), precision=highest)
    partial_b = jnp.einsum("kjr,kr->jr", along_i, time_init, precision=highest)
    metric_b = gram_a * gram_time
    summed_b = lax.psum_scatter(partial_b, "gx", scatter_dimension=0, tiled=True)
    raw_b = solve_rows(metric_b, summed_b)
    gram_raw_b = lax.psum(gram_of(raw_b), ("gx", "gy"))
    norm_b, gram_b = scaled(gram_raw_b)
    mine_b = raw_b / norm_b
    block_b = lax.all_gather(mine_b, "gx", axis=0, tiled=True)
    again_j = lax.dot_general(tensor, block_b, (((2,), (0,)), ((), ())), precision=highest)
    partial_c = jnp.einsum("kir,ir->kr", again_j, block_a, precision=highest)
    summed_c = lax.psum(partial_c, ("gx", "gy"))
    time_factor = solve_rows(gram_a * gram_b, summed_c)
    scale_a = jnp.sqrt(jnp.float32(rows_first * devices_x))
    scale_b = jnp.sqrt(jnp.float32(rows_second * devices_y))
    return (mine_a * scale_a, mine_b * scale_b, time_factor)


def solution(mesh):
    return jax.shard_map(
        shards,
        mesh=mesh,
        in_specs=(P(None, "gx", "gy"), P(("gy", "gx"), None), P()),
        out_specs=(P(("gx", "gy"), None), P(("gy", "gx"), None), P()),
        check_vma=False,
    )
```

profile of v0, /device:TPU:1, one launch (start us, length us, event | category | flops | bytes accessed | tf_op | source)
XLA Modules:
  0.0 1219.1 jit_solution(17560255353868017815)
XLA Ops:
  7.2 1.7 fusion.29
  9.0 21.8 %all_gather.9 = f32[384,128]{1,0:T(8,128)S(1)} all-gather(f32[24,128]{1,0:T(8,128)} %param.7), channel_id=1, replica_groups=mesh['gx'=16,'gy'=16] {'gx'}, dimensions={0}, use_global_device_ids=true | all-gather | bytes 208896 | tf_op jit(solution)/shard_map/all_gather | solution.py:31
  30.8 10.7 multiply_reduce_fusion
  41.5 0.8 copy.38
  42.4 0.6 dynamic-slice
  43.6 211.8 %all-reduce.8.cloned.1.call-done = f32[128,128]{0,1:T(8,128)} async-done(((f32[128,128]{0,1:T(8,128)}), f32[128,128]{0,1:T(8,128)}) %all-reduce.8.cloned.1.call-update) | async-done | bytes 65552 | tf_op jit(solution)/shard_map/psum | solution.py:30
  255.4 1.1 fusion.28
  256.7 11.7 cholesky.59
  268.4 0.6 compare_reduce_fusion.2
  269.1 0.7 fusion.6
  269.8 9.8 custom-call.20
  279.6 120.3 %all-reduce.14.cloned.1.call-done = f32[384,128]{0,1:T(8,128)} async-done(((f32[384,128]{0,1:T(8,128)}), f32[384,128]{0,1:T(8,128)}) %all-reduce.14.cloned.1.call-update) | async-done | bytes 196624
  399.9 1.2 fusion.10
  401.1 0.2 fusion.20
  401.3 0.9 fusion.30
  402.3 0.2 all-reduce.16.cloned.1.call-start
  402.5 0.6 dynamic-slice.2
  403.9 247.8 %all-reduce.10.cloned.1.call-done = f32[128,128]{0,1:T(8,128)} async-done(((f32[128,128]{0,1:T(8,128)}), f32[128,128]{0,1:T(8,128)}) %all-reduce.10.cloned.1.call-update) | async-done | bytes 65552 | tf_op jit(solution)/shard_map/psum | solution.py:37
  651.7 1.9 gather_fusion
  653.6 0.6 broadcast_multiply_fusion.1
  654.2 0.9 fusion.24
  655.3 11.7 cholesky.70
  667.0 0.6 compare_reduce_fusion.1
  667.7 31.7 %all_gather.10 = f32[384,128]{1,0:T(8,128)S(1)} all-gather(f32[24,128]{1,0:T(8,128)S(1)} %get-tuple-element.8), channel_id=1, replica_groups=mesh['gx'=16,'gy'=16] {'gy'}, dimensions={0}, use_global_device_ids=true | all-gather | bytes 208896 | tf_op jit(solution)/shard_map/all_gather | solution.py:40
  699.4 8.3 convolution_bitcast_fusion.1
  707.7 3.9 fusion.2
  711.5 0.7 copy.57
  712.2 0.3 all-reduce.12.cloned.1.call-start
  712.5 0.7 fusion.7
  713.2 9.8 custom-call.21
  723.0 107.7 %all-reduce.16.cloned.1.call-done = f32[384,128]{0,1:T(8,128)} async-done(((f32[384,128]{0,1:T(8,128)}), f32[384,128]{0,1:T(8,128)}) %all-reduce.16.cloned.1.call-update) | async-done | bytes 196624
  830.7 1.2 fusion.9
  831.9 0.2 fusion.16
  832.1 0.9 fusion.31
  833.3 240.3 %all-reduce.12.cloned.1.call-done = f32[128,128]{0,1:T(8,128)} async-done(((f32[128,128]{0,1:T(8,128)}), f32[128,128]{0,1:T(8,128)}) %all-reduce.12.cloned.1.call-update) | async-done | bytes 65552 | tf_op jit(solution)/shard_map/psum | solution.py:46
  1073.5 1.9 gather_fusion.1
  1075.5 0.6 broadcast_multiply_fusion
  1076.1 0.9 divide_multiply_fusion
  1077.2 11.7 cholesky.81
  1088.9 0.6 compare_reduce_fusion
  1089.6 0.7 fusion.8
  1090.2 9.8 custom-call.14
  1100.0 19.4 %all_gather.11 = f32[384,128]{1,0:T(8,128)S(1)} all-gather(f32[24,128]{1,0:T(8,128)S(1)} %get-tuple-element.6), channel_id=1, replica_groups=mesh['gx'=16,'gy'=16] {'gx'}, dimensions={0}, use_global_device_ids=true | all-gather | bytes 208896 | tf_op jit(solution)/shard_map/all_gather | solution.py:49
  1119.4 12.2 %convolution_bitcast_fusion = f32[16,384,128]{1,2,0:T(8,128)S(1)} fusion(f32[16,384,384]{2,1,0:T(8,128)} %param.6, f32[384,128]{1,0:T(8,128)S(1)} %all_gather.11), kind=kOutput, calls=%fused_computation.7 | convolution fusion | flops 3623878656 | bytes 12779520 | tf_op jit(solution)/shard_map/dot_general | solution.py:50
  1131.7 5.8 fusion
  1137.5 73.6 %psum.31 = f32[16,128]{0,1:T(8,128)S(1)} all-reduce(f32[16,128]{0,1:T(8,128)S(1)} %bitcast.100), channel_id=1, replica_groups=mesh['gx'=16,'gy'=16] {'gx','gy'}, use_global_device_ids=true, to_apply=%region_7.10 | all-reduce | flops 2048 | bytes 16384 | tf_op jit(solution)/shard_map/psum | solution.py:52
  1211.1 0.2 fusion.13
  1211.3 0.9 fusion.11
  (30 shorter events, 0.9 us)
Async XLA Ops:
  7.2 248.3 %all-reduce.8.cloned.1.call-start = ((), (), s32[]{:S(2)}) async-start(), calls=%async_computation | async-start | bytes 131072 | tf_op jit(solution)/shard_map/psum | solution.py:30
  8.9 391.0 %all-reduce.14.cloned.1.call-start = ((), (), s32[]{:S(2)}) async-start(), calls=%async_computation.3 | async-start | bytes 393216
  30.8 11.6 copy-start.3
  30.8 224.7 %copy-start.1 = (f32[16,128]{1,0:T(8,128)S(1)}, f32[16,128]{1,0:T(8,128)}, u32[]{:S(2)}) copy-start(f32[16,128]{1,0:T(8,128)} %param.8) | copy-start | bytes 24580
  30.8 371.7 %copy-start.2 = (u32[256]{0:T(256)S(1)}, u32[256]{0:T(256)}, u32[]{:S(2)}) copy-start(u32[256]{0:T(256)} %constant.93) | copy-start | bytes 3076
  42.3 609.4 %all-reduce.10.cloned.1.call-start = ((), (), s32[]{:S(2)}) async-start(), calls=%async_computation.1 | async-start | bytes 131072 | tf_op jit(solution)/shard_map/psum | solution.py:37
  402.3 428.4 %all-reduce.16.cloned.1.call-start = ((), (), s32[]{:S(2)}) async-start(), calls=%async_computation.4 | async-start | bytes 393216
  707.6 368.4 %copy-start = (f32[128,128]{0,1:T(8,128)S(1)}, f32[128,128]{0,1:T(8,128)}, u32[]{:S(2)}) copy-start(f32[128,128]{0,1:T(8,128)} %all-reduce.10.cloned.1.call-done) | copy-start | bytes 196612
  712.2 361.3 %all-reduce.12.cloned.1.call-start = ((), (), s32[]{:S(2)}) async-start(), calls=%async_computation.2 | async-start | bytes 131072 | tf_op jit(solution)/shard_map/psum | solution.py:46
Sparse Core Ops, SparseCore 0:
  13.5 241.8 all-reduce.7
  258.1 141.7 all-reduce.13
  406.3 245.3 all-reduce.9
  712.4 118.2 all-reduce.15
  836.0 237.4 all-reduce.11
where the time goes:
time: 1230 us; the launch traced here: 1220 us
  waiting for transfers between devices  928 us (75%)
  blocking collectives  147 us (12%)
  other arithmetic  71.7 us (6%)
  matrix products  49.5 us (4%)
  between operations  15.8 us (1%)
    psum x1, waiting for transfers between devices, shards(): gram_raw_a = lax.psum(gram_of(raw_a), ('gx', 'gy'))  248 us
    psum x1, waiting for transfers between devices, shards(): gram_raw_b = lax.psum(gram_of(raw_b), ('gx', 'gy'))  240 us
    unnamed x7, waiting for transfers between devices  228 us
    psum x1, waiting for transfers between devices, shards(): gram_old = lax.psum(gram_of(factor_b_init), ('gx', 'gy'))  212 us
    psum x1, blocking collectives, shards(): summed_c = lax.psum(partial_c, ('gx', 'gy'))  73.6 us
    another operation x9, other arithmetic, solve_rows(): lower = jnp.linalg.cholesky(metric)  37.2 us
    all_gather x1, blocking collectives, shards(): block_a = lax.all_gather(mine_a, 'gy', axis=0, tiled=True)  31.7 us
    another operation x6, other arithmetic, solve_rows(): return jax.scipy.linalg.cho_solve((lower, True), rhs.T).T  31.4 us
  transfers between devices with their start and end apart: 5, of which 5 were waited for; matrix products, arithmetic and copies ran while one was open for 4% of the time, Pallas kernels for 0%

commit v1 on v0

v1 whole, which is shorter than its diff:
```python
import functools

import jax
import jax.numpy as jnp
from jax import lax
from jax.experimental import pallas as pl
from jax.experimental.pallas import tpu as pltpu
from jax.sharding import PartitionSpec as P

highest = lax.Precision.HIGHEST
epsilon = 1e-06
f32 = jnp.float32
bf16 = jnp.bfloat16
VMEM = pltpu.VMEM
TILE = 8


def split(x):
    high = x.astype(bf16)
    return high, (x - high.astype(f32)).astype(bf16)


def dot(a, b, ca, cb, precision=highest):
    return lax.dot_general(a, b, (((ca,), (cb,)), ((), ())), precision=precision, preferred_element_type=f32)


def raw_dot(a, b, ca, cb):
    return lax.dot_general(a, b, (((ca,), (cb,)), ((), ())), preferred_element_type=f32)


def spd_inverse(matrix):
    n = matrix.shape[0]
    blocks = n // TILE
    rows = [matrix[TILE * v : TILE * (v + 1), :] for v in range(blocks)]
    lane = lax.broadcasted_iota(jnp.int32, (TILE, n), 1)
    sub = lax.broadcasted_iota(jnp.int32, (TILE, n), 0)

    def column(value, at):
        return jnp.broadcast_to(value[:, at : at + 1], (TILE, n))

    def row(value, at):
        return jnp.broadcast_to(value[at : at + 1, :], (TILE, n))

    for block in range(blocks):
        first = TILE * block
        inside = (lane >= first) & (lane < first + TILE)
        panel = rows[block]
        columns = [column(panel, first + s) for s in range(TILE)]
        b = [[row(columns[s], i) for s in range(i + 1)] for i in range(TILE)]
        start = jnp.where(inside, jnp.where(lane - first == sub, 1.0, 0.0), panel)
        p = [row(start, i) for i in range(TILE)]
        inverse = []
        for j in range(TILE):
            inverse.append(1.0 / b[j][j])
            for i in range(j + 1, TILE):
                factor = b[i][j] * inverse[j]
                for t in range(j + 1, i + 1):
                    b[i][t] = b[i][t] - factor * b[t][j]
                p[i] = p[i] - factor * p[j]
        solved = [None] * TILE
        for j in reversed(range(TILE)):
            value = p[j]
            for i in range(j + 1, TILE):
                value = value - b[i][j] * solved[i]
            solved[j] = value * inverse[j]
        update = []
        for v in range(blocks):
            if v == block:
                value = solved[TILE - 1]
                for s in range(TILE - 1):
                    value = jnp.where(sub == s, solved[s], value)
            else:
                value = jnp.where(inside, 0.0, rows[v])
                for s in range(TILE):
                    value = value - column(rows[v], first + s) * solved[s]
            update.append(value)
        rows = update
    return jnp.concatenate(rows, axis=0)


def diagonal(matrix):
    n = matrix.shape[0]
    same = lax.broadcasted_iota(jnp.int32, (n, n), 0) == lax.broadcasted_iota(jnp.int32, (n, n), 1)
    kept = jnp.where(same, matrix, 0.0)
    return jnp.sum(kept, axis=0, keepdims=True), jnp.sum(kept, axis=1, keepdims=True)


def scaled(gram_raw):
    across, down = diagonal(gram_raw)
    norm_row, norm_column = jnp.sqrt(across + epsilon), jnp.sqrt(down + epsilon)
    return norm_row, norm_column, gram_raw / (norm_column * norm_row)


def unpack(ref, at, size):
    return jnp.concatenate([ref[s, at : at + size, :] for s in range(ref.shape[0])], axis=0)


def first_product(tensor_ref, factor_ref, time_ref, out_ref):
    factor = unpack(factor_ref, 0, factor_ref.shape[1])
    rank = factor.shape[1]
    high, low = split(factor)
    both = jnp.concatenate([high, low], axis=1)
    snapshots = tensor_ref.shape[0]
    total = jnp.zeros((tensor_ref.shape[1], rank), f32)
    for k in range(snapshots):
        t_high, t_low = split(tensor_ref[k])
        product = raw_dot(t_high, both, 1, 0)
        along = product[:, :rank] + product[:, rank:] + raw_dot(t_low, high, 1, 0)
        total = total + along * time_ref[k : k + 1, :]
    gram = dot(factor, factor, 0, 0)
    pack(out_ref, total, gram)


def pack(out_ref, total, gram):
    parts = out_ref.shape[0]
    rows, extra = total.shape[0] // parts, gram.shape[0] // parts
    for d in range(parts):
        out_ref[d, :rows, :] = total[d * rows : (d + 1) * rows]
        out_ref[d, rows:, :] = gram[d * extra : (d + 1) * extra]


def sum_and_copy(in_ref, out_ref):
    total = jnp.sum(in_ref[...], axis=0)
    for d in range(out_ref.shape[0]):
        out_ref[d] = total


def second_product(tensor_ref, in_ref, time_ref, out_ref, along_ref, raw_ref):
    rank = time_ref.shape[1]
    rows = in_ref.shape[1] - rank // in_ref.shape[0]
    time = time_ref[...]
    gram_time = dot(time, time, 0, 0)
    metric = unpack(in_ref, rows, in_ref.shape[1] - rows) * gram_time
    raw = dot(unpack(in_ref, 0, rows), spd_inverse(metric), 1, 0)
    raw_ref[...] = raw
    gram = dot(raw, raw, 0, 0)
    turned = raw.T
    high, low = split(turned)
    both = jnp.concatenate([high, low], axis=0)
    time_turned = time.T
    total = jnp.zeros((rank, tensor_ref.shape[2]), f32)
    for k in range(tensor_ref.shape[0]):
        t_high, t_low = split(tensor_ref[k])
        product = raw_dot(both, t_high, 1, 0)
        along = product[:rank] + product[rank:] + raw_dot(high, t_low, 1, 0)
        along_ref[k] = along
        total = total + along * time_turned[:, k : k + 1]
    pack(out_ref, total.T, gram)


def third_product(in_ref, along_ref, time_ref, out_ref, raw_ref, gram_ref, norm_ref):
    snapshots, rank = time_ref.shape
    rows = in_ref.shape[1] - rank // in_ref.shape[0]
    time = time_ref[...]
    gram_time = dot(time, time, 0, 0)
    norm_row, norm_column, gram_a = scaled(unpack(in_ref, rows, in_ref.shape[1] - rows))
    raw = dot(unpack(in_ref, 0, rows) / norm_row, spd_inverse(gram_a * gram_time), 1, 0)
    raw_ref[...] = raw
    gram_ref[...] = gram_a
    norm_ref[...] = norm_row
    turned = raw.T
    lane = lax.broadcasted_iota(jnp.int32, (rank, rank), 1)
    sums = jnp.zeros((rank, rank), f32)
    for k in range(snapshots):
        part = jnp.sum(along_ref[k] * turned, axis=1, keepdims=True)
        sums = jnp.where(lane == k, part, sums)
    products = (sums / norm_column).T[:snapshots]
    gram = dot(raw, raw, 0, 0)
    extra = rank // in_ref.shape[0]
    mine = gram_slice(gram, lax.axis_index("gx"), extra)
    for d in range(out_ref.shape[0]):
        out_ref[d, :snapshots, :] = products
        out_ref[d, snapshots:, :] = mine


def gram_slice(gram, index, extra):
    value = gram[:extra]
    for s in range(1, gram.shape[0] // extra):
        value = jnp.where(index == s, gram[s * extra : (s + 1) * extra], value)
    return value


def finish(size_a, size_b, in_ref, gram_a_ref, norm_a_ref, raw_a_ref, raw_b_ref, factor_a_ref, factor_b_ref, time_ref):
    snapshots = time_ref.shape[0]
    norm_row, _, gram_b = scaled(unpack(in_ref, snapshots, in_ref.shape[1] - snapshots))
    products = jnp.sum(in_ref[:, :snapshots, :], axis=0) / norm_row
    time_ref[...] = dot(products, spd_inverse(gram_a_ref[...] * gram_b), 1, 0)
    rows_a, rows_b = factor_a_ref.shape[0], factor_b_ref.shape[0]
    at_a = pl.multiple_of(lax.axis_index("gy") * rows_a, TILE)
    at_b = pl.multiple_of(lax.axis_index("gx") * rows_b, TILE)
    factor_a_ref[...] = raw_a_ref[pl.ds(at_a, rows_a), :] / norm_a_ref[...] * jnp.sqrt(f32(size_a))
    factor_b_ref[...] = raw_b_ref[pl.ds(at_b, rows_b), :] / norm_row * jnp.sqrt(f32(size_b))


def call(kernel, inputs, outputs, name, limit=48 << 20):
    shapes = [jax.ShapeDtypeStruct(s, f32) for s in outputs]
    single = len(shapes) == 1
    space = pl.BlockSpec(memory_space=VMEM)
    return pl.pallas_call(
        kernel,
        out_shape=shapes[0] if single else shapes,
        in_specs=[space] * len(inputs),
        out_specs=space if single else [space] * len(shapes),
        compiler_params=pltpu.CompilerParams(vmem_limit_bytes=limit),
        name=name,
    )(*inputs)


def exchange(value, axis):
    return lax.all_to_all(value, axis, 0, 0)


def shards(tensor, factor_b_init, time_init):
    nx, ny = lax.axis_size("gx"), lax.axis_size("gy")
    snapshots, rank = time_init.shape
    rows_i, rows_j = tensor.shape[1], tensor.shape[2]
    own_i, own_j = rows_i // ny, rows_j // nx
    extra_x, extra_y = rank // nx, rank // ny
    block_b = exchange(jnp.broadcast_to(factor_b_init[None], (nx,) + factor_b_init.shape), "gx")
    sent = call(first_product, (tensor, block_b, time_init), [(ny, own_i + extra_y, rank)], "first_product")
    sent = exchange(sent, "gy")
    sent = call(sum_and_copy, (sent,), [sent.shape], "sum_a")
    sent = exchange(sent, "gy")
    sent, along, raw_a = call(
        second_product,
        (tensor, sent, time_init),
        [(nx, own_j + extra_x, rank), (snapshots, rank, rows_j), (rows_i, rank)],
        "second_product",
    )
    sent = exchange(sent, "gx")
    sent = call(sum_and_copy, (sent,), [sent.shape], "sum_b")
    sent = exchange(sent, "gx")
    sent, raw_b, gram_a, norm_a = call(
        third_product,
        (sent, along, time_init),
        [(ny, snapshots + extra_x, rank), (rows_j, rank), (rank, rank), (1, rank)],
        "third_product",
    )
    sent = exchange(sent, "gy")
    sent = call(sum_and_copy, (sent,), [(nx,) + sent.shape[1:]], "sum_c")
    sent = exchange(sent, "gx")
    return call(
        functools.partial(finish, rows_i * nx, rows_j * ny),
        (sent, gram_a, norm_a, raw_a, raw_b),
        [(own_i, rank), (own_j, rank), (snapshots, rank)],
        "finish",
    )


def solution(mesh):
    return jax.shard_map(
        lambda *arrays: tuple(shards(*arrays)),
        mesh=mesh,
        in_specs=(P(None, "gx", "gy"), P(("gy", "gx"), None), P()),
        out_specs=(P(("gx", "gy"), None), P(("gy", "gx"), None), P()),
        check_vma=False,
    )
```

time: 1230 us -> 141 us (0.11)
  waiting for transfers between devices: 928 us -> 0 us
  other arithmetic: 71.7 us -> 0 us
  matrix products: 49.5 us -> 0 us
  blocking collectives: 147 us -> 99.9 us
  Pallas kernels: 0 us -> 38.1 us
  between operations: 15.8 us -> 0.68 us
    psum x3 -> x0, waiting for transfers between devices: 700 us -> none  [the longest x1 248 us: shards(): gram_raw_a = lax.psum(gram_of(raw_a), ('gx', 'gy'))]
    unnamed x7 -> x0, waiting for transfers between devices: 228 us -> none
    all_to_all x0 -> x7, blocking collectives: none -> 99.9 us  [exchange(): return lax.all_to_all(value, axis, 0, 0)]
    psum x1 -> x0, blocking collectives: 73.6 us -> none  [shards(): summed_c = lax.psum(partial_c, ('gx', 'gy'))]
    all_gather x3 -> x0, blocking collectives: 72.9 us -> none  [the longest x1 31.7 us: shards(): block_a = lax.all_gather(mine_a, 'gy', axis=0, tiled=True)]
    another operation x15 -> x0, other arithmetic: 68.6 us -> none  [the longest x9 37.2 us: solve_rows(): lower = jnp.linalg.cholesky(metric)]
    dot_general x9 -> x0, matrix products: 45.5 us -> none  [the longest x1 12.2 us: shards(): lax.dot_general(tensor, block_b, (((2,), (0,)), ((), ())), precision=high...]
    pallas_call x0 -> x7, Pallas kernels: none -> 38.1 us  [call(): pl.pallas_call(kernel, out_shape=shapes[0] if single else shapes, in_spec...]
  transfers between devices with their start and end apart: 5 -> 0, of which waited for: 5 -> 0; matrix products, arithmetic and copies ran while one was open for 4% -> 0% of each run, Pallas kernels for 0% -> 0%
where the time goes in v1:
time: 141 us; the launch traced here: 140 us
  blocking collectives  99.9 us (71%)
  Pallas kernels  38.1 us (27%)
  local copies, waits for them, and re-layouts  1.43 us (1%)
    all_to_all x7, blocking collectives, exchange(): return lax.all_to_all(value, axis, 0, 0)  99.9 us
    pallas_call x7, Pallas kernels, call(): pl.pallas_call(kernel, out_shape=shapes[0] if single else shapes, in_spec...  38.1 us

profile of v1, /device:TPU:1, one launch (start us, length us, event | category | flops | bytes accessed | tf_op | source)
XLA Modules:
  0.0 140.2 jit_solution(2015536345760779376)
XLA Ops:
  0.6 0.0 copy-start.1
  0.6 0.7 broadcast_in_dim.2
  1.4 13.4 %all_to_all.35.factor_ref = f32[16,24,128]{2,1,0:T(8,128)S(1)} all-to-all(f32[16,24,128]{2,1,0:T(8,128)S(1)} %broadcast_in_dim.2), channel_id=1, replica_groups=mesh['gx'=16,'gy'=16] {'gx'}, dimensions={0} | all-to-all | bytes 393216 | tf_op jit(solution)/shard_map/all_to_all | solution.py:210
  14.8 0.0 copy-start
  14.8 0.7 copy-done
  15.5 6.9 %first_product.1 = f32[16,32,128]{2,1,0:T(8,128)S(1)} custom-call(f32[16,384,384]{2,1,0:T(8,128)} %tensor_ref.3, f32[16,24,128]{2,1,0:T(8,128)S(1)} %all_to_all.35.factor_ref, f32[16,128]{1,0:T(8,128)S(1)} %copy-done), custom_call_target="tpu_custom_call" | custom-call | tf_op jit(solution)/shard_map/first_product/pallas_call | solution.py:199
  22.4 22.9 %all_to_all.36.in_ref = f32[16,32,128]{2,1,0:T(8,128)S(1)} all-to-all(f32[16,32,128]{2,1,0:T(8,128)S(1)} %first_product.1), channel_id=1, replica_groups=mesh['gx'=16,'gy'=16] {'gy'}, dimensions={0} | all-to-all | bytes 524288 | tf_op jit(solution)/shard_map/all_to_all | solution.py:210
  45.3 14.8 %all_to_all.37.in_ref = f32[16,32,128]{2,1,0:T(8,128)S(1)} all-to-all(f32[16,32,128]{2,1,0:T(8,128)S(1)} %sum_a.1), channel_id=1, replica_groups=mesh['gx'=16,'gy'=16] {'gy'}, dimensions={0} | all-to-all | bytes 524288 | tf_op jit(solution)/shard_map/all_to_all | solution.py:210
  60.1 0.0 copy-done.1
  60.1 16.9 %second_product.1 = (f32[16,32,128]{2,1,0:T(8,128)S(1)}, f32[16,128,384]{2,1,0:T(8,128)S(1)}, f32[384,128]{1,0:T(8,128)S(1)}) custom-call(f32[16,384,384]{2,1,0:T(8,128)} %tensor_ref.3, f32[16,32,128]{2,1,0:T(8,128)S(1)} %all_to_all.37.in_ref, f32[16,128]{1,0:T(8,128)S(1)} %copy-done.1), custom_call_target="tpu_custom_call" | custom-call | tf_op jit(solution)/shard_map/second_product/pallas_call | solution.py:199
  77.0 13.0 %all_to_all.38.in_ref = f32[16,32,128]{2,1,0:T(8,128)S(1)} all-to-all(f32[16,32,128]{2,1,0:T(8,128)S(1)} %get-tuple-element.10), channel_id=1, replica_groups=mesh['gx'=16,'gy'=16] {'gx'}, dimensions={0} | all-to-all | bytes 524288 | tf_op jit(solution)/shard_map/all_to_all | solution.py:210
  90.0 10.3 %all_to_all.39.in_ref = f32[16,32,128]{2,1,0:T(8,128)S(1)} all-to-all(f32[16,32,128]{2,1,0:T(8,128)S(1)} %sum_b.1), channel_id=1, replica_groups=mesh['gx'=16,'gy'=16] {'gx'}, dimensions={0} | all-to-all | bytes 524288 | tf_op jit(solution)/shard_map/all_to_all | solution.py:210
  100.3 7.9 %third_product.1 = (f32[16,24,128]{2,1,0:T(8,128)S(1)}, f32[384,128]{1,0:T(8,128)S(1)}, f32[128,128]{1,0:T(8,128)S(1)}, f32[1,128]{1,0:T(1,128)S(1)}) custom-call(f32[16,32,128]{2,1,0:T(8,128)S(1)} %all_to_all.39.in_ref, f32[16,128,384]{2,1,0:T(8,128)S(1)} %get-tuple-element.11.along_ref, f32[16,128]{1,0:T(8,128)S(1)} %copy-done.1), custom_call_target="tpu_custom_call" | custom-call | tf_op jit(solution)/shard_map/third_product/pallas_call | solution.py:199
  108.1 14.0 %all_to_all.40.in_ref = f32[16,24,128]{2,1,0:T(8,128)S(1)} all-to-all(f32[16,24,128]{2,1,0:T(8,128)S(1)} %get-tuple-element.12), channel_id=1, replica_groups=mesh['gx'=16,'gy'=16] {'gy'}, dimensions={0} | all-to-all | bytes 393216 | tf_op jit(solution)/shard_map/all_to_all | solution.py:210
  122.1 11.6 %all_to_all.41.in_ref = f32[16,24,128]{2,1,0:T(8,128)S(1)} all-to-all(f32[16,24,128]{2,1,0:T(8,128)S(1)} %sum_c.1), channel_id=1, replica_groups=mesh['gx'=16,'gy'=16] {'gx'}, dimensions={0} | all-to-all | bytes 393216 | tf_op jit(solution)/shard_map/all_to_all | solution.py:210
  133.7 6.4 %finish.1 = (f32[24,128]{1,0:T(8,128)}, f32[24,128]{1,0:T(8,128)}, f32[16,128]{1,0:T(8,128)}) custom-call(f32[16,24,128]{2,1,0:T(8,128)S(1)} %all_to_all.41.in_ref, f32[128,128]{1,0:T(8,128)S(1)} %get-tuple-element.13.gram_a_ref, f32[1,128]{1,0:T(1,128)S(1)} %get-tuple-element.14.norm_a_ref, f32[384,128]{1,0:T(8,128)S(1)} %get-tuple-element.15.raw_a_ref, ...), custom_call_target="tpu_custom_call" | custom-call | tf_op jit(solution)/shard_map/finish/pallas_call | solution.py:199
  (3 shorter events, 0.1 us)
Async XLA Ops:
  0.6 59.5 %copy-start.1 = (f32[16,128]{1,0:T(8,128)S(1)}, f32[16,128]{1,0:T(8,128)}, u32[]{:S(2)}) copy-start(f32[16,128]{1,0:T(8,128)} %time_ref.5) | copy-start | bytes 24580
  14.8 0.7 copy-start

commit v2 on v1

--- a/solution.py
+++ b/solution.py
@@ -13,6 +13,7 @@
 bf16 = jnp.bfloat16
 VMEM = pltpu.VMEM
 TILE = 8
+PAIR = 2
 
 
 def split(x):
@@ -36,7 +37,7 @@
     sub = lax.broadcasted_iota(jnp.int32, (TILE, n), 0)
 
     def column(value, at):
-        return jnp.broadcast_to(value[:, at : at + 1], (TILE, n))
+        return jnp.take_along_axis(value, jnp.full((TILE, n), at, jnp.int32), axis=1)
 
     def row(value, at):
         return jnp.broadcast_to(value[at : at + 1, :], (TILE, n))
@@ -85,6 +86,12 @@
     return jnp.sum(kept, axis=0, keepdims=True), jnp.sum(kept, axis=1, keepdims=True)
 
 
+def metric_inverse(metric):
+    across, down = diagonal(metric)
+    scale = lax.rsqrt(across) * lax.rsqrt(down)
+    return spd_inverse(metric * scale) * scale
+
+
 def scaled(gram_raw):
     across, down = diagonal(gram_raw)
     norm_row, norm_column = jnp.sqrt(across + epsilon), jnp.sqrt(down + epsilon)
@@ -95,18 +102,31 @@
     return jnp.concatenate([ref[s, at : at + size, :] for s in range(ref.shape[0])], axis=0)
 
 
-def first_product(tensor_ref, factor_ref, time_ref, out_ref):
+def spread(factor_ref, time_ref, out_ref, time_out_ref):
+    for d in range(out_ref.shape[0]):
+        out_ref[d] = factor_ref[...]
+    time_out_ref[...] = time_ref[...]
+
+
+def first_product(tensor_ref, factor_ref, time_ref, out_ref, high_ref, low_ref, held, arrived):
+    copies = [pltpu.make_async_copy(tensor_ref.at[k], held.at[k], arrived.at[k]) for k in range(held.shape[0])]
+    for copy in copies:
+        copy.start()
     factor = unpack(factor_ref, 0, factor_ref.shape[1])
-    rank = factor.shape[1]
-    high, low = split(factor)
-    both = jnp.concatenate([high, low], axis=1)
-    snapshots = tensor_ref.shape[0]
+    columns, rank = factor.shape
     total = jnp.zeros((tensor_ref.shape[1], rank), f32)
-    for k in range(snapshots):
-        t_high, t_low = split(tensor_ref[k])
+    for first in range(0, time_ref.shape[0], PAIR):
+        weights = jnp.concatenate([factor * time_ref[k : k + 1, :] for k in range(first, first + PAIR)], axis=0)
+        high, low = split(weights)
+        both = jnp.concatenate([high, low], axis=1)
+        for k in range(first, first + PAIR):
+            copies[k].wait()
+        t_high, t_low = split(jnp.concatenate([held[k] for k in range(first, first + PAIR)], axis=1))
+        at = first * columns
+        high_ref[:, at : at + PAIR * columns] = t_high
+        low_ref[:, at : at + PAIR * columns] = t_low
         product = raw_dot(t_high, both, 1, 0)
-        along = product[:, :rank] + product[:, rank:] + raw_dot(t_low, high, 1, 0)
-        total = total + along * time_ref[k : k + 1, :]
+        total = total + (product[:, :rank] + product[:, rank:] + raw_dot(t_low, high, 1, 0))
     gram = dot(factor, factor, 0, 0)
     pack(out_ref, total, gram)
 
@@ -125,26 +145,29 @@
         out_ref[d] = total
 
 
-def second_product(tensor_ref, in_ref, time_ref, out_ref, along_ref, raw_ref):
-    rank = time_ref.shape[1]
+def second_product(high_ref, low_ref, in_ref, time_ref, out_ref, along_ref, raw_ref):
+    snapshots, rank = time_ref.shape
     rows = in_ref.shape[1] - rank // in_ref.shape[0]
     time = time_ref[...]
     gram_time = dot(time, time, 0, 0)
     metric = unpack(in_ref, rows, in_ref.shape[1] - rows) * gram_time
-    raw = dot(unpack(in_ref, 0, rows), spd_inverse(metric), 1, 0)
+    raw = dot(unpack(in_ref, 0, rows), metric_inverse(metric), 1, 0)
     raw_ref[...] = raw
-    gram = dot(raw, raw, 0, 0)
     turned = raw.T
+    gram = dot(turned, raw, 1, 0)
     high, low = split(turned)
     both = jnp.concatenate([high, low], axis=0)
     time_turned = time.T
-    total = jnp.zeros((rank, tensor_ref.shape[2]), f32)
-    for k in range(tensor_ref.shape[0]):
-        t_high, t_low = split(tensor_ref[k])
-        product = raw_dot(both, t_high, 1, 0)
-        along = product[:rank] + product[rank:] + raw_dot(high, t_low, 1, 0)
-        along_ref[k] = along
-        total = total + along * time_turned[:, k : k + 1]
+    columns = high_ref.shape[1] // snapshots
+    wide = PAIR * columns
+    total = jnp.zeros((rank, columns), f32)
+    for first in range(0, snapshots, PAIR):
+        at = first * columns
+        product = raw_dot(both, high_ref[:, at : at + wide], 1, 0)
+        along = product[:rank] + product[rank:] + raw_dot(high, low_ref[:, at : at + wide], 1, 0)
+        along_ref[:, at : at + wide] = along
+        for k in range(PAIR):
+            total = total + along[:, k * columns : (k + 1) * columns] * time_turned[:, first + k : first + k + 1]
     pack(out_ref, total.T, gram)
 
 
@@ -154,18 +177,19 @@
     time = time_ref[...]
     gram_time = dot(time, time, 0, 0)
     norm_row, norm_column, gram_a = scaled(unpack(in_ref, rows, in_ref.shape[1] - rows))
-    raw = dot(unpack(in_ref, 0, rows) / norm_row, spd_inverse(gram_a * gram_time), 1, 0)
+    raw = dot(unpack(in_ref, 0, rows) / norm_row, metric_inverse(gram_a * gram_time), 1, 0)
     raw_ref[...] = raw
     gram_ref[...] = gram_a
     norm_ref[...] = norm_row
     turned = raw.T
+    columns = raw.shape[0]
     lane = lax.broadcasted_iota(jnp.int32, (rank, rank), 1)
     sums = jnp.zeros((rank, rank), f32)
     for k in range(snapshots):
-        part = jnp.sum(along_ref[k] * turned, axis=1, keepdims=True)
+        part = jnp.sum(along_ref[:, k * columns : (k + 1) * columns] * turned, axis=1, keepdims=True)
         sums = jnp.where(lane == k, part, sums)
     products = (sums / norm_column).T[:snapshots]
-    gram = dot(raw, raw, 0, 0)
+    gram = dot(turned, raw, 1, 0)
     extra = rank // in_ref.shape[0]
     mine = gram_slice(gram, lax.axis_index("gx"), extra)
     for d in range(out_ref.shape[0]):
@@ -184,7 +208,7 @@
     snapshots = time_ref.shape[0]
     norm_row, _, gram_b = scaled(unpack(in_ref, snapshots, in_ref.shape[1] - snapshots))
     products = jnp.sum(in_ref[:, :snapshots, :], axis=0) / norm_row
-    time_ref[...] = dot(products, spd_inverse(gram_a_ref[...] * gram_b), 1, 0)
+    time_ref[...] = dot(products, metric_inverse(gram_a_ref[...] * gram_b), 1, 0)
     rows_a, rows_b = factor_a_ref.shape[0], factor_b_ref.shape[0]
     at_a = pl.multiple_of(lax.axis_index("gy") * rows_a, TILE)
     at_b = pl.multiple_of(lax.axis_index("gx") * rows_b, TILE)
@@ -192,15 +216,16 @@
     factor_b_ref[...] = raw_b_ref[pl.ds(at_b, rows_b), :] / norm_row * jnp.sqrt(f32(size_b))
 
 
-def call(kernel, inputs, outputs, name, limit=48 << 20):
-    shapes = [jax.ShapeDtypeStruct(s, f32) for s in outputs]
+def call(kernel, inputs, outputs, name, spaces=None, scratch=(), limit=16 << 20):
+    shapes = [o if isinstance(o, jax.ShapeDtypeStruct) else jax.ShapeDtypeStruct(o, f32) for o in outputs]
     single = len(shapes) == 1
     space = pl.BlockSpec(memory_space=VMEM)
     return pl.pallas_call(
         kernel,
         out_shape=shapes[0] if single else shapes,
-        in_specs=[space] * len(inputs),
+        in_specs=spaces or [space] * len(inputs),
         out_specs=space if single else [space] * len(shapes),
+        scratch_shapes=scratch,
         compiler_params=pltpu.CompilerParams(vmem_limit_bytes=limit),
         name=name,
     )(*inputs)
@@ -216,15 +241,26 @@
     rows_i, rows_j = tensor.shape[1], tensor.shape[2]
     own_i, own_j = rows_i // ny, rows_j // nx
     extra_x, extra_y = rank // nx, rank // ny
-    block_b = exchange(jnp.broadcast_to(factor_b_init[None], (nx,) + factor_b_init.shape), "gx")
-    sent = call(first_product, (tensor, block_b, time_init), [(ny, own_i + extra_y, rank)], "first_product")
+    block_b, time = call(spread, (factor_b_init, time_init), [(nx,) + factor_b_init.shape, time_init.shape], "spread")
+    block_b = exchange(block_b, "gx")
+    half = jax.ShapeDtypeStruct((rows_i, snapshots * rows_j), bf16)
+    space = pl.BlockSpec(memory_space=VMEM)
+    sent, high, low = call(
+        first_product,
+        (tensor, block_b, time),
+        [(ny, own_i + extra_y, rank), half, half],
+        "first_product",
+        [pl.BlockSpec(memory_space=pl.ANY), space, space],
+        [VMEM(tensor.shape, f32), pltpu.SemaphoreType.DMA((snapshots,))],
+        42 << 20,
+    )
     sent = exchange(sent, "gy")
     sent = call(sum_and_copy, (sent,), [sent.shape], "sum_a")
     sent = exchange(sent, "gy")
     sent, along, raw_a = call(
         second_product,
-        (tensor, sent, time_init),
-        [(nx, own_j + extra_x, rank), (snapshots, rank, rows_j), (rows_i, rank)],
+        (high, low, sent, time),
+        [(nx, own_j + extra_x, rank), (rank, snapshots * rows_j), (rows_i, rank)],
         "second_product",
     )
     sent = exchange(sent, "gx")
@@ -232,7 +268,7 @@
     sent = exchange(sent, "gx")
     sent, raw_b, gram_a, norm_a = call(
         third_product,
-        (sent, along, time_init),
+        (sent, along, time),
         [(ny, snapshots + extra_x, rank), (rows_j, rank), (rank, rank), (1, rank)],
         "third_product",
     )

time: 141 us -> 126 us (0.89)
  Pallas kernels: 38.1 us -> 23.2 us
    pallas_call x7 -> x8, Pallas kernels: 38.1 us -> 23.2 us  [call(): pl.pallas_call(kernel, out_shape=shapes[0] if single else shapes, in_spec...]
where the time goes in v2:
time: 126 us; the launch traced here: 125 us
  blocking collectives  99.9 us (79%)
  Pallas kernels  23.2 us (18%)
  local copies, waits for them, and re-layouts  1.4 us (1%)
    all_to_all x7, blocking collectives, exchange(): return lax.all_to_all(value, axis, 0, 0)  99.9 us
    pallas_call x8, Pallas kernels, call(): pl.pallas_call(kernel, out_shape=shapes[0] if single else shapes, in_spec...  23.2 us

profile of v2, /device:TPU:1, one launch (start us, length us, event | category | flops | bytes accessed | tf_op | source)
XLA Modules:
  0.0 125.3 jit_solution(17210343641398248715)
XLA Ops:
  0.6 0.0 copy-start
  0.6 0.7 copy-done
  1.3 0.0 copy-start.1
  1.3 0.7 copy-done.1
  2.1 13.4 %all_to_all.35.factor_ref = f32[16,24,128]{2,1,0:T(8,128)S(1)} all-to-all(f32[16,24,128]{2,1,0:T(8,128)S(1)} %get-tuple-element.15), channel_id=1, replica_groups=mesh['gx'=16,'gy'=16] {'gx'}, dimensions={0} | all-to-all | bytes 393216 | tf_op jit(solution)/shard_map/all_to_all | solution.py:235
  15.5 5.7 %first_product.1 = (f32[16,32,128]{2,1,0:T(8,128)S(1)}, bf16[384,6144]{1,0:T(8,128)(2,1)S(1)}, bf16[384,6144]{1,0:T(8,128)(2,1)S(1)}) custom-call(f32[16,384,384]{2,1,0:T(8,128)} %tensor_ref.1, f32[16,24,128]{2,1,0:T(8,128)S(1)} %all_to_all.35.factor_ref, f32[16,128]{1,0:T(8,128)S(1)} %get-tuple-element.16.time_ref), custom_call_target="tpu_custom_call" | custom-call | tf_op jit(solution)/shard_map/first_product/pallas_call | solution.py:223
  21.2 22.9 %all_to_all.36.in_ref = f32[16,32,128]{2,1,0:T(8,128)S(1)} all-to-all(f32[16,32,128]{2,1,0:T(8,128)S(1)} %get-tuple-element.19), channel_id=1, replica_groups=mesh['gx'=16,'gy'=16] {'gy'}, dimensions={0} | all-to-all | bytes 524288 | tf_op jit(solution)/shard_map/all_to_all | solution.py:235
  44.1 14.8 %all_to_all.37.in_ref = f32[16,32,128]{2,1,0:T(8,128)S(1)} all-to-all(f32[16,32,128]{2,1,0:T(8,128)S(1)} %sum_a.1), channel_id=1, replica_groups=mesh['gx'=16,'gy'=16] {'gy'}, dimensions={0} | all-to-all | bytes 524288 | tf_op jit(solution)/shard_map/all_to_all | solution.py:235
  58.9 7.7 %second_product.1 = (f32[16,32,128]{2,1,0:T(8,128)S(1)}, f32[128,6144]{1,0:T(8,128)S(1)}, f32[384,128]{1,0:T(8,128)S(1)}) custom-call(bf16[384,6144]{1,0:T(8,128)(2,1)S(1)} %get-tuple-element.17.high_ref, bf16[384,6144]{1,0:T(8,128)(2,1)S(1)} %get-tuple-element.18.low_ref, f32[16,32,128]{2,1,0:T(8,128)S(1)} %all_to_all.37.in_ref, ...), custom_call_target="tpu_custom_call" | custom-call | tf_op jit(solution)/shard_map/second_product/pallas_call | solution.py:223
  66.6 13.0 %all_to_all.38.in_ref = f32[16,32,128]{2,1,0:T(8,128)S(1)} all-to-all(f32[16,32,128]{2,1,0:T(8,128)S(1)} %get-tuple-element.20), channel_id=1, replica_groups=mesh['gx'=16,'gy'=16] {'gx'}, dimensions={0} | all-to-all | bytes 524288 | tf_op jit(solution)/shard_map/all_to_all | solution.py:235
  79.6 10.3 %all_to_all.39.in_ref = f32[16,32,128]{2,1,0:T(8,128)S(1)} all-to-all(f32[16,32,128]{2,1,0:T(8,128)S(1)} %sum_b.1), channel_id=1, replica_groups=mesh['gx'=16,'gy'=16] {'gx'}, dimensions={0} | all-to-all | bytes 524288 | tf_op jit(solution)/shard_map/all_to_all | solution.py:235
  89.9 5.0 %third_product.1 = (f32[16,24,128]{2,1,0:T(8,128)S(1)}, f32[384,128]{1,0:T(8,128)S(1)}, f32[128,128]{1,0:T(8,128)S(1)}, f32[1,128]{1,0:T(1,128)S(1)}) custom-call(f32[16,32,128]{2,1,0:T(8,128)S(1)} %all_to_all.39.in_ref, f32[128,6144]{1,0:T(8,128)S(1)} %get-tuple-element.21.along_ref, f32[16,128]{1,0:T(8,128)S(1)} %get-tuple-element.16.time_ref), custom_call_target="tpu_custom_call" | custom-call | tf_op jit(solution)/shard_map/third_product/pallas_call | solution.py:223
  94.9 14.0 %all_to_all.40.in_ref = f32[16,24,128]{2,1,0:T(8,128)S(1)} all-to-all(f32[16,24,128]{2,1,0:T(8,128)S(1)} %get-tuple-element.22), channel_id=1, replica_groups=mesh['gx'=16,'gy'=16] {'gy'}, dimensions={0} | all-to-all | bytes 393216 | tf_op jit(solution)/shard_map/all_to_all | solution.py:235
  109.0 11.6 %all_to_all.41.in_ref = f32[16,24,128]{2,1,0:T(8,128)S(1)} all-to-all(f32[16,24,128]{2,1,0:T(8,128)S(1)} %sum_c.1), channel_id=1, replica_groups=mesh['gx'=16,'gy'=16] {'gx'}, dimensions={0} | all-to-all | bytes 393216 | tf_op jit(solution)/shard_map/all_to_all | solution.py:235
  120.5 4.7 %finish.1 = (f32[24,128]{1,0:T(8,128)}, f32[24,128]{1,0:T(8,128)}, f32[16,128]{1,0:T(8,128)}) custom-call(f32[16,24,128]{2,1,0:T(8,128)S(1)} %all_to_all.41.in_ref, f32[128,128]{1,0:T(8,128)S(1)} %get-tuple-element.23.gram_a_ref, f32[1,128]{1,0:T(1,128)S(1)} %get-tuple-element.24.norm_a_ref, f32[384,128]{1,0:T(8,128)S(1)} %get-tuple-element.25.raw_a_ref, ...), custom_call_target="tpu_custom_call" | custom-call | tf_op jit(solution)/shard_map/finish/pallas_call | solution.py:223
  (4 shorter events, 0.1 us)
Async XLA Ops:
  0.6 0.7 copy-start
  1.3 0.7 copy-start.1

commit v3 on v2

--- a/solution.py
+++ b/solution.py
@@ -14,6 +14,7 @@
 VMEM = pltpu.VMEM
 TILE = 8
 PAIR = 2
+LOOK = 2
 
 
 def split(x):
@@ -27,6 +28,13 @@
 
 def raw_dot(a, b, ca, cb):
     return lax.dot_general(a, b, (((ca,), (cb,)), ((), ())), preferred_element_type=f32)
+
+
+def three_parts(x):
+    high = x.astype(bf16)
+    rest = x - high.astype(f32)
+    middle = rest.astype(bf16)
+    return high, middle, (rest - middle.astype(f32)).astype(bf16)
 
 
 def spd_inverse(matrix):
@@ -35,6 +43,7 @@
     rows = [matrix[TILE * v : TILE * (v + 1), :] for v in range(blocks)]
     lane = lax.broadcasted_iota(jnp.int32, (TILE, n), 1)
     sub = lax.broadcasted_iota(jnp.int32, (TILE, n), 0)
+    zero = jnp.zeros((TILE, n), f32)
 
     def column(value, at):
         return jnp.take_along_axis(value, jnp.full((TILE, n), at, jnp.int32), axis=1)
@@ -64,17 +73,30 @@
             for i in range(j + 1, TILE):
                 value = value - b[i][j] * solved[i]
             solved[j] = value * inverse[j]
+        result = solved[TILE - 1]
+        for s in range(TILE - 1):
+            result = jnp.where(sub == s, solved[s], result)
+        c_high, c_middle, c_low = three_parts(jnp.concatenate(rows, axis=0))
+        padded = jnp.concatenate([result if v == block else zero for v in range(blocks)], axis=0)
+        r_high, r_middle, r_low = three_parts(padded)
+        pair = jnp.concatenate([r_high, r_middle], axis=1)
+        large = raw_dot(jnp.concatenate([c_high, c_middle], axis=1), jnp.concatenate([pair, pair], axis=0), 1, 0)
+        small = raw_dot(jnp.concatenate([c_high, c_low], axis=1), jnp.concatenate([r_low, r_high], axis=0), 1, 0)
+        product = large[:, :n] + (large[:, n:] + small)
+        near = [(block + 1 + q) % blocks for q in range(LOOK)]
         update = []
         for v in range(blocks):
             if v == block:
-                value = solved[TILE - 1]
-                for s in range(TILE - 1):
-                    value = jnp.where(sub == s, solved[s], value)
+                update.append(result)
+                continue
+            if v in near:
+                terms = [column(rows[v], first + s) * solved[s] for s in range(TILE)]
+                while len(terms) > 1:
+                    terms = [terms[q] + terms[q + 1] for q in range(0, len(terms), 2)]
+                change = terms[0]
             else:
-                value = jnp.where(inside, 0.0, rows[v])
-                for s in range(TILE):
-                    value = value - column(rows[v], first + s) * solved[s]
-            update.append(value)
+                change = product[TILE * v : TILE * (v + 1), :]
+            update.append(jnp.where(inside, 0.0, rows[v]) - change)
         rows = update
     return jnp.concatenate(rows, axis=0)
 
@@ -102,16 +124,12 @@
     return jnp.concatenate([ref[s, at : at + size, :] for s in range(ref.shape[0])], axis=0)
 
 
-def spread(factor_ref, time_ref, out_ref, time_out_ref):
+def spread(factor_ref, out_ref):
     for d in range(out_ref.shape[0]):
         out_ref[d] = factor_ref[...]
-    time_out_ref[...] = time_ref[...]
-
-
-def first_product(tensor_ref, factor_ref, time_ref, out_ref, high_ref, low_ref, held, arrived):
-    copies = [pltpu.make_async_copy(tensor_ref.at[k], held.at[k], arrived.at[k]) for k in range(held.shape[0])]
-    for copy in copies:
-        copy.start()
+
+
+def first_product(tensor_ref, factor_ref, time_ref, out_ref, high_ref, low_ref):
     factor = unpack(factor_ref, 0, factor_ref.shape[1])
     columns, rank = factor.shape
     total = jnp.zeros((tensor_ref.shape[1], rank), f32)
@@ -119,9 +137,7 @@
         weights = jnp.concatenate([factor * time_ref[k : k + 1, :] for k in range(first, first + PAIR)], axis=0)
         high, low = split(weights)
         both = jnp.concatenate([high, low], axis=1)
-        for k in range(first, first + PAIR):
-            copies[k].wait()
-        t_high, t_low = split(jnp.concatenate([held[k] for k in range(first, first + PAIR)], axis=1))
+        t_high, t_low = split(jnp.concatenate([tensor_ref[k] for k in range(first, first + PAIR)], axis=1))
         at = first * columns
         high_ref[:, at : at + PAIR * columns] = t_high
         low_ref[:, at : at + PAIR * columns] = t_low
@@ -216,7 +232,7 @@
     factor_b_ref[...] = raw_b_ref[pl.ds(at_b, rows_b), :] / norm_row * jnp.sqrt(f32(size_b))
 
 
-def call(kernel, inputs, outputs, name, spaces=None, scratch=(), limit=16 << 20):
+def call(kernel, inputs, outputs, name, spaces=None, scratch=(), limit=16 << 20, cost=None):
     shapes = [o if isinstance(o, jax.ShapeDtypeStruct) else jax.ShapeDtypeStruct(o, f32) for o in outputs]
     single = len(shapes) == 1
     space = pl.BlockSpec(memory_space=VMEM)
@@ -226,6 +242,7 @@
         in_specs=spaces or [space] * len(inputs),
         out_specs=space if single else [space] * len(shapes),
         scratch_shapes=scratch,
+        cost_estimate=cost,
         compiler_params=pltpu.CompilerParams(vmem_limit_bytes=limit),
         name=name,
     )(*inputs)
@@ -241,25 +258,23 @@
     rows_i, rows_j = tensor.shape[1], tensor.shape[2]
     own_i, own_j = rows_i // ny, rows_j // nx
     extra_x, extra_y = rank // nx, rank // ny
-    block_b, time = call(spread, (factor_b_init, time_init), [(nx,) + factor_b_init.shape, time_init.shape], "spread")
+    behind = pl.CostEstimate(flops=5 * 10**9, bytes_accessed=2 * factor_b_init.size * 4 * nx, transcendentals=0)
+    block_b = call(spread, (factor_b_init,), [(nx,) + factor_b_init.shape], "spread", cost=behind)
     block_b = exchange(block_b, "gx")
     half = jax.ShapeDtypeStruct((rows_i, snapshots * rows_j), bf16)
-    space = pl.BlockSpec(memory_space=VMEM)
     sent, high, low = call(
         first_product,
-        (tensor, block_b, time),
+        (tensor, block_b, time_init),
         [(ny, own_i + extra_y, rank), half, half],
         "first_product",
-        [pl.BlockSpec(memory_space=pl.ANY), space, space],
-        [VMEM(tensor.shape, f32), pltpu.SemaphoreType.DMA((snapshots,))],
-        42 << 20,
+        limit=16 << 20,
     )
     sent = exchange(sent, "gy")
     sent = call(sum_and_copy, (sent,), [sent.shape], "sum_a")
     sent = exchange(sent, "gy")
     sent, along, raw_a = call(
         second_product,
-        (high, low, sent, time),
+        (high, low, sent, time_init),
         [(nx, own_j + extra_x, rank), (rank, snapshots * rows_j), (rows_i, rank)],
         "second_product",
     )
@@ -268,7 +283,7 @@
     sent = exchange(sent, "gx")
     sent, raw_b, gram_a, norm_a = call(
         third_product,
-        (sent, along, time),
+        (sent, along, time_init),
         [(ny, snapshots + extra_x, rank), (rows_j, rank), (rank, rank), (1, rank)],
         "third_product",
     )

time: 126 us -> 122 us (0.968)
  Pallas kernels: 23.2 us -> 20.1 us
    pallas_call x8, Pallas kernels: 23.2 us -> 20.1 us  [call(): pl.pallas_call(kernel, out_shape=shapes[0] if single else shapes, in_spec...]
where the time goes in v3:
time: 122 us
  blocking collectives  100 us (82%)
  Pallas kernels  20.1 us (16%)
    all_to_all x7, blocking collectives, exchange(): return lax.all_to_all(value, axis, 0, 0)  100 us
    pallas_call x8, Pallas kernels, call(): pl.pallas_call(kernel, out_shape=shapes[0] if single else shapes, in_spec...  20.1 us

profile of v3, /device:TPU:1, one launch (start us, length us, event | category | flops | bytes accessed | tf_op | source)
XLA Modules:
  0.0 121.7 jit_solution(61074115780513999)
XLA Ops:
  0.6 0.0 copy-start.1
  0.6 0.0 copy-start.2
  0.7 0.7 copy-done.2
  1.4 0.0 copy-start
  1.4 13.7 %all_to_all.35.factor_ref = f32[16,24,128]{2,1,0:T(8,128)S(1)} all-to-all(f32[16,24,128]{2,1,0:T(8,128)S(1)} %spread.1), channel_id=1, replica_groups=mesh['gx'=16,'gy'=16] {'gx'}, dimensions={0} | all-to-all | bytes 393216 | tf_op jit(solution)/shard_map/all_to_all | solution.py:252
  15.0 0.0 copy-done.1
  15.0 0.0 copy-done
  15.1 3.4 %first_product.1 = (f32[16,32,128]{2,1,0:T(8,128)S(1)}, bf16[384,6144]{1,0:T(8,128)(2,1)S(1)}, bf16[384,6144]{1,0:T(8,128)(2,1)S(1)}) custom-call(f32[16,384,384]{2,1,0:T(8,128)S(1)} %copy-done, f32[16,24,128]{2,1,0:T(8,128)S(1)} %all_to_all.35.factor_ref, f32[16,128]{1,0:T(8,128)S(1)} %copy-done.1), custom_call_target="tpu_custom_call" | custom-call | tf_op jit(solution)/shard_map/first_product/pallas_call | solution.py:239
  18.4 22.9 %all_to_all.36.in_ref = f32[16,32,128]{2,1,0:T(8,128)S(1)} all-to-all(f32[16,32,128]{2,1,0:T(8,128)S(1)} %get-tuple-element.15), channel_id=1, replica_groups=mesh['gx'=16,'gy'=16] {'gy'}, dimensions={0} | all-to-all | bytes 524288 | tf_op jit(solution)/shard_map/all_to_all | solution.py:252
  41.4 14.8 %all_to_all.37.in_ref = f32[16,32,128]{2,1,0:T(8,128)S(1)} all-to-all(f32[16,32,128]{2,1,0:T(8,128)S(1)} %sum_a.1), channel_id=1, replica_groups=mesh['gx'=16,'gy'=16] {'gy'}, dimensions={0} | all-to-all | bytes 524288 | tf_op jit(solution)/shard_map/all_to_all | solution.py:252
  56.2 7.3 %second_product.1 = (f32[16,32,128]{2,1,0:T(8,128)S(1)}, f32[128,6144]{1,0:T(8,128)S(1)}, f32[384,128]{1,0:T(8,128)S(1)}) custom-call(bf16[384,6144]{1,0:T(8,128)(2,1)S(1)} %get-tuple-element.13.high_ref, bf16[384,6144]{1,0:T(8,128)(2,1)S(1)} %get-tuple-element.14.low_ref, f32[16,32,128]{2,1,0:T(8,128)S(1)} %all_to_all.37.in_ref, f32[16,128]{1,0:T(8,128)S(1)} %copy-done.1), custom_call_target="tpu_custom_call" | custom-call | tf_op jit(solution)/shard_map/second_product/pallas_call | solution.py:239
  63.5 13.0 %all_to_all.38.in_ref = f32[16,32,128]{2,1,0:T(8,128)S(1)} all-to-all(f32[16,32,128]{2,1,0:T(8,128)S(1)} %get-tuple-element.16), channel_id=1, replica_groups=mesh['gx'=16,'gy'=16] {'gx'}, dimensions={0} | all-to-all | bytes 524288 | tf_op jit(solution)/shard_map/all_to_all | solution.py:252
  76.5 10.3 %all_to_all.39.in_ref = f32[16,32,128]{2,1,0:T(8,128)S(1)} all-to-all(f32[16,32,128]{2,1,0:T(8,128)S(1)} %sum_b.1), channel_id=1, replica_groups=mesh['gx'=16,'gy'=16] {'gx'}, dimensions={0} | all-to-all | bytes 524288 | tf_op jit(solution)/shard_map/all_to_all | solution.py:252
  86.8 4.8 %third_product.1 = (f32[16,24,128]{2,1,0:T(8,128)S(1)}, f32[384,128]{1,0:T(8,128)S(1)}, f32[128,128]{1,0:T(8,128)S(1)}, f32[1,128]{1,0:T(1,128)S(1)}) custom-call(f32[16,32,128]{2,1,0:T(8,128)S(1)} %all_to_all.39.in_ref, f32[128,6144]{1,0:T(8,128)S(1)} %get-tuple-element.17.along_ref, f32[16,128]{1,0:T(8,128)S(1)} %copy-done.1), custom_call_target="tpu_custom_call" | custom-call | tf_op jit(solution)/shard_map/third_product/pallas_call | solution.py:239
  91.6 14.0 %all_to_all.40.in_ref = f32[16,24,128]{2,1,0:T(8,128)S(1)} all-to-all(f32[16,24,128]{2,1,0:T(8,128)S(1)} %get-tuple-element.18), channel_id=1, replica_groups=mesh['gx'=16,'gy'=16] {'gy'}, dimensions={0} | all-to-all | bytes 393216 | tf_op jit(solution)/shard_map/all_to_all | solution.py:252
  105.7 11.6 %all_to_all.41.in_ref = f32[16,24,128]{2,1,0:T(8,128)S(1)} all-to-all(f32[16,24,128]{2,1,0:T(8,128)S(1)} %sum_c.1), channel_id=1, replica_groups=mesh['gx'=16,'gy'=16] {'gx'}, dimensions={0} | all-to-all | bytes 393216 | tf_op jit(solution)/shard_map/all_to_all | solution.py:252
  117.2 4.5 %finish.1 = (f32[24,128]{1,0:T(8,128)}, f32[24,128]{1,0:T(8,128)}, f32[16,128]{1,0:T(8,128)}) custom-call(f32[16,24,128]{2,1,0:T(8,128)S(1)} %all_to_all.41.in_ref, f32[128,128]{1,0:T(8,128)S(1)} %get-tuple-element.19.gram_a_ref, f32[1,128]{1,0:T(1,128)S(1)} %get-tuple-element.20.norm_a_ref, f32[384,128]{1,0:T(8,128)S(1)} %get-tuple-element.21.raw_a_ref, ...), custom_call_target="tpu_custom_call" | custom-call | tf_op jit(solution)/shard_map/finish/pallas_call | solution.py:239
  (4 shorter events, 0.1 us)
Async XLA Ops:
  0.6 14.4 %copy-start.1 = (f32[16,128]{1,0:T(8,128)S(1)}, f32[16,128]{1,0:T(8,128)}, u32[]{:S(2)}) copy-start(f32[16,128]{1,0:T(8,128)} %time_ref.5) | copy-start | bytes 24580
  0.6 0.7 copy-start.2
  1.4 13.7 %copy-start = (f32[16,384,384]{2,1,0:T(8,128)S(1)}, f32[16,384,384]{2,1,0:T(8,128)}, u32[]{:S(2)}) copy-start(f32[16,384,384]{2,1,0:T(8,128)} %tensor_ref.1) | copy-start | bytes 28311556

commit v4 on v3

--- a/solution.py
+++ b/solution.py
@@ -77,8 +77,10 @@
         for s in range(TILE - 1):
             result = jnp.where(sub == s, solved[s], result)
         c_high, c_middle, c_low = three_parts(jnp.concatenate(rows, axis=0))
-        padded = jnp.concatenate([result if v == block else zero for v in range(blocks)], axis=0)
-        r_high, r_middle, r_low = three_parts(padded)
+        r_high, r_middle, r_low = [
+            jnp.concatenate([part.astype(f32) if v == block else zero for v in range(blocks)], axis=0).astype(bf16)
+            for part in three_parts(result)
+        ]
         pair = jnp.concatenate([r_high, r_middle], axis=1)
         large = raw_dot(jnp.concatenate([c_high, c_middle], axis=1), jnp.concatenate([pair, pair], axis=0), 1, 0)
         small = raw_dot(jnp.concatenate([c_high, c_low], axis=1), jnp.concatenate([r_low, r_high], axis=0), 1, 0)
@@ -108,16 +110,17 @@
     return jnp.sum(kept, axis=0, keepdims=True), jnp.sum(kept, axis=1, keepdims=True)
 
 
-def metric_inverse(metric):
-    across, down = diagonal(metric)
-    scale = lax.rsqrt(across) * lax.rsqrt(down)
-    return spd_inverse(metric * scale) * scale
+def metric_inverse(one, other, one_diagonal, other_diagonal):
+    across, down = [lax.rsqrt(p * q) for p, q in zip(one_diagonal, other_diagonal)]
+    scale = down * across
+    return spd_inverse(one * other * scale) * scale
 
 
 def scaled(gram_raw):
     across, down = diagonal(gram_raw)
     norm_row, norm_column = jnp.sqrt(across + epsilon), jnp.sqrt(down + epsilon)
-    return norm_row, norm_column, gram_raw / (norm_column * norm_row)
+    ends = across / (norm_row * norm_row), down / (norm_column * norm_column)
+    return norm_row, norm_column, gram_raw / (norm_column * norm_row), ends
 
 
 def unpack(ref, at, size):
@@ -129,7 +132,7 @@
         out_ref[d] = factor_ref[...]
 
 
-def first_product(tensor_ref, factor_ref, time_ref, out_ref, high_ref, low_ref):
+def first_product(tensor_ref, factor_ref, time_ref, out_ref, high_ref, low_ref, gram_time_ref):
     factor = unpack(factor_ref, 0, factor_ref.shape[1])
     columns, rank = factor.shape
     total = jnp.zeros((tensor_ref.shape[1], rank), f32)
@@ -145,6 +148,7 @@
         total = total + (product[:, :rank] + product[:, rank:] + raw_dot(t_low, high, 1, 0))
     gram = dot(factor, factor, 0, 0)
     pack(out_ref, total, gram)
+    gram_time_ref[...] = dot(time_ref[...], time_ref[...], 0, 0)
 
 
 def pack(out_ref, total, gram):
@@ -161,19 +165,17 @@
         out_ref[d] = total
 
 
-def second_product(high_ref, low_ref, in_ref, time_ref, out_ref, along_ref, raw_ref):
+def second_product(high_ref, low_ref, in_ref, time_ref, gram_time_ref, out_ref, along_ref, raw_ref):
     snapshots, rank = time_ref.shape
     rows = in_ref.shape[1] - rank // in_ref.shape[0]
-    time = time_ref[...]
-    gram_time = dot(time, time, 0, 0)
-    metric = unpack(in_ref, rows, in_ref.shape[1] - rows) * gram_time
-    raw = dot(unpack(in_ref, 0, rows), metric_inverse(metric), 1, 0)
-    raw_ref[...] = raw
-    turned = raw.T
-    gram = dot(turned, raw, 1, 0)
+    gram_old, gram_time = unpack(in_ref, rows, in_ref.shape[1] - rows), gram_time_ref[...]
+    inverse = metric_inverse(gram_old, gram_time, diagonal(gram_old), diagonal(gram_time))
+    turned = dot(inverse, unpack(in_ref, 0, rows), 1, 1)
+    raw_ref[...] = dot(in_ref[lax.axis_index("gy"), :rows, :], inverse, 1, 1)
+    gram = dot(turned, turned, 1, 1)
     high, low = split(turned)
     both = jnp.concatenate([high, low], axis=0)
-    time_turned = time.T
+    time_turned = time_ref[...].T
     columns = high_ref.shape[1] // snapshots
     wide = PAIR * columns
     total = jnp.zeros((rank, columns), f32)
@@ -187,26 +189,26 @@
     pack(out_ref, total.T, gram)
 
 
-def third_product(in_ref, along_ref, time_ref, out_ref, raw_ref, gram_ref, norm_ref):
-    snapshots, rank = time_ref.shape
-    rows = in_ref.shape[1] - rank // in_ref.shape[0]
-    time = time_ref[...]
-    gram_time = dot(time, time, 0, 0)
-    norm_row, norm_column, gram_a = scaled(unpack(in_ref, rows, in_ref.shape[1] - rows))
-    raw = dot(unpack(in_ref, 0, rows) / norm_row, metric_inverse(gram_a * gram_time), 1, 0)
-    raw_ref[...] = raw
+def third_product(in_ref, along_ref, gram_time_ref, out_ref, raw_ref, gram_ref, norm_ref):
+    rank = gram_time_ref.shape[0]
+    extra = rank // in_ref.shape[0]
+    rows = in_ref.shape[1] - extra
+    snapshots = out_ref.shape[1] - extra
+    norm_row, norm_column, gram_a, ends = scaled(unpack(in_ref, rows, extra))
+    gram_time = gram_time_ref[...]
+    inverse = metric_inverse(gram_a, gram_time, ends, diagonal(gram_time))
+    turned = dot(inverse, unpack(in_ref, 0, rows) / norm_row, 1, 1)
+    raw_ref[...] = dot(in_ref[lax.axis_index("gx"), :rows, :] / norm_row, inverse, 1, 1)
     gram_ref[...] = gram_a
     norm_ref[...] = norm_row
-    turned = raw.T
-    columns = raw.shape[0]
+    gram = dot(turned, turned, 1, 1)
+    columns = turned.shape[1]
     lane = lax.broadcasted_iota(jnp.int32, (rank, rank), 1)
     sums = jnp.zeros((rank, rank), f32)
     for k in range(snapshots):
         part = jnp.sum(along_ref[:, k * columns : (k + 1) * columns] * turned, axis=1, keepdims=True)
         sums = jnp.where(lane == k, part, sums)
     products = (sums / norm_column).T[:snapshots]
-    gram = dot(turned, raw, 1, 0)
-    extra = rank // in_ref.shape[0]
     mine = gram_slice(gram, lax.axis_index("gx"), extra)
     for d in range(out_ref.shape[0]):
         out_ref[d, :snapshots, :] = products
@@ -222,14 +224,12 @@
 
 def finish(size_a, size_b, in_ref, gram_a_ref, norm_a_ref, raw_a_ref, raw_b_ref, factor_a_ref, factor_b_ref, time_ref):
     snapshots = time_ref.shape[0]
-    norm_row, _, gram_b = scaled(unpack(in_ref, snapshots, in_ref.shape[1] - snapshots))
+    norm_row, _, gram_b, ends = scaled(unpack(in_ref, snapshots, in_ref.shape[1] - snapshots))
+    gram_a = gram_a_ref[...]
     products = jnp.sum(in_ref[:, :snapshots, :], axis=0) / norm_row
-    time_ref[...] = dot(products, metric_inverse(gram_a_ref[...] * gram_b), 1, 0)
-    rows_a, rows_b = factor_a_ref.shape[0], factor_b_ref.shape[0]
-    at_a = pl.multiple_of(lax.axis_index("gy") * rows_a, TILE)
-    at_b = pl.multiple_of(lax.axis_index("gx") * rows_b, TILE)
-    factor_a_ref[...] = raw_a_ref[pl.ds(at_a, rows_a), :] / norm_a_ref[...] * jnp.sqrt(f32(size_a))
-    factor_b_ref[...] = raw_b_ref[pl.ds(at_b, rows_b), :] / norm_row * jnp.sqrt(f32(size_b))
+    time_ref[...] = dot(products, metric_inverse(gram_b, gram_a, ends, diagonal(gram_a)), 1, 0)
+    factor_a_ref[...] = raw_a_ref[...] / norm_a_ref[...] * jnp.sqrt(f32(size_a))
+    factor_b_ref[...] = raw_b_ref[...] / norm_row * jnp.sqrt(f32(size_b))
 
 
 def call(kernel, inputs, outputs, name, spaces=None, scratch=(), limit=16 << 20, cost=None):
@@ -262,10 +262,10 @@
     block_b = call(spread, (factor_b_init,), [(nx,) + factor_b_init.shape], "spread", cost=behind)
     block_b = exchange(block_b, "gx")
     half = jax.ShapeDtypeStruct((rows_i, snapshots * rows_j), bf16)
-    sent, high, low = call(
+    sent, high, low, gram_time = call(
         first_product,
         (tensor, block_b, time_init),
-        [(ny, own_i + extra_y, rank), half, half],
+        [(ny, own_i + extra_y, rank), half, half, (rank, rank)],
         "first_product",
         limit=16 << 20,
     )
@@ -274,8 +274,8 @@
     sent = exchange(sent, "gy")
     sent, along, raw_a = call(
         second_product,
-        (high, low, sent, time_init),
-        [(nx, own_j + extra_x, rank), (rank, snapshots * rows_j), (rows_i, rank)],
+        (high, low, sent, time_init, gram_time),
+        [(nx, own_j + extra_x, rank), (rank, snapshots * rows_j), (own_i, rank)],
         "second_product",
     )
     sent = exchange(sent, "gx")
@@ -283,8 +283,8 @@
     sent = exchange(sent, "gx")
     sent, raw_b, gram_a, norm_a = call(
         third_product,
-        (sent, along, time_init),
-        [(ny, snapshots + extra_x, rank), (rows_j, rank), (rank, rank), (1, rank)],
+        (sent, along, gram_time),
+        [(ny, snapshots + extra_x, rank), (own_j, rank), (rank, rank), (1, rank)],
         "third_product",
     )
     sent = exchange(sent, "gy")

time: 122 us -> 121 us (level)
  no operation moved by 1% of the time
where the time goes in v4:
time: 121 us
  blocking collectives  100 us (83%)
  Pallas kernels  19.3 us (16%)
    all_to_all x7, blocking collectives, exchange(): return lax.all_to_all(value, axis, 0, 0)  100 us
    pallas_call x8, Pallas kernels, call(): pl.pallas_call(kernel, out_shape=shapes[0] if single else shapes, in_spec...  19.3 us

profile of v4, /device:TPU:1, one launch (start us, length us, event | category | flops | bytes accessed | tf_op | source)
XLA Modules:
  0.0 120.9 jit_solution(15107489676567880209)
XLA Ops:
  0.6 0.0 copy-start.1
  0.6 0.0 copy-start.2
  0.7 0.7 copy-done.2
  1.4 0.0 copy-start
  1.4 13.7 %all_to_all.35.factor_ref = f32[16,24,128]{2,1,0:T(8,128)S(1)} all-to-all(f32[16,24,128]{2,1,0:T(8,128)S(1)} %spread.1), channel_id=1, replica_groups=mesh['gx'=16,'gy'=16] {'gx'}, dimensions={0} | all-to-all | bytes 393216 | tf_op jit(solution)/shard_map/all_to_all | solution.py:252
  15.0 0.0 copy-done.1
  15.0 0.0 copy-done
  15.1 3.1 %first_product.1 = (f32[16,32,128]{2,1,0:T(8,128)S(1)}, bf16[384,6144]{1,0:T(8,128)(2,1)S(1)}, bf16[384,6144]{1,0:T(8,128)(2,1)S(1)}, f32[128,128]{1,0:T(8,128)S(1)}) custom-call(f32[16,384,384]{2,1,0:T(8,128)S(1)} %copy-done, f32[16,24,128]{2,1,0:T(8,128)S(1)} %all_to_all.35.factor_ref, f32[16,128]{1,0:T(8,128)S(1)} %copy-done.1), custom_call_target="tpu_custom_call" | custom-call | tf_op jit(solution)/shard_map/first_product/pallas_call | solution.py:239
  18.1 22.9 %all_to_all.36.in_ref = f32[16,32,128]{2,1,0:T(8,128)S(1)} all-to-all(f32[16,32,128]{2,1,0:T(8,128)S(1)} %get-tuple-element.16), channel_id=1, replica_groups=mesh['gx'=16,'gy'=16] {'gy'}, dimensions={0} | all-to-all | bytes 524288 | tf_op jit(solution)/shard_map/all_to_all | solution.py:252
  41.1 14.8 %all_to_all.37.in_ref = f32[16,32,128]{2,1,0:T(8,128)S(1)} all-to-all(f32[16,32,128]{2,1,0:T(8,128)S(1)} %sum_a.1), channel_id=1, replica_groups=mesh['gx'=16,'gy'=16] {'gy'}, dimensions={0} | all-to-all | bytes 524288 | tf_op jit(solution)/shard_map/all_to_all | solution.py:252
  55.9 7.1 %second_product.1 = (f32[16,32,128]{2,1,0:T(8,128)S(1)}, f32[128,6144]{1,0:T(8,128)S(1)}, f32[24,128]{1,0:T(8,128)S(1)}) custom-call(bf16[384,6144]{1,0:T(8,128)(2,1)S(1)} %get-tuple-element.14.high_ref, bf16[384,6144]{1,0:T(8,128)(2,1)S(1)} %get-tuple-element.15.low_ref, f32[16,32,128]{2,1,0:T(8,128)S(1)} %all_to_all.37.in_ref, f32[16,128]{1,0:T(8,128)S(1)} %copy-done.1, ...), custom_call_target="tpu_custom_call" | custom-call | tf_op jit(solution)/shard_map/second_product/pallas_call | solution.py:239
  63.0 13.0 %all_to_all.38.in_ref = f32[16,32,128]{2,1,0:T(8,128)S(1)} all-to-all(f32[16,32,128]{2,1,0:T(8,128)S(1)} %get-tuple-element.18), channel_id=1, replica_groups=mesh['gx'=16,'gy'=16] {'gx'}, dimensions={0} | all-to-all | bytes 524288 | tf_op jit(solution)/shard_map/all_to_all | solution.py:252
  76.0 10.3 %all_to_all.39.in_ref = f32[16,32,128]{2,1,0:T(8,128)S(1)} all-to-all(f32[16,32,128]{2,1,0:T(8,128)S(1)} %sum_b.1), channel_id=1, replica_groups=mesh['gx'=16,'gy'=16] {'gx'}, dimensions={0} | all-to-all | bytes 524288 | tf_op jit(solution)/shard_map/all_to_all | solution.py:252
  86.3 4.5 %third_product.1 = (f32[16,24,128]{2,1,0:T(8,128)S(1)}, f32[24,128]{1,0:T(8,128)S(1)}, f32[128,128]{1,0:T(8,128)S(1)}, f32[1,128]{1,0:T(1,128)S(1)}) custom-call(f32[16,32,128]{2,1,0:T(8,128)S(1)} %all_to_all.39.in_ref, f32[128,6144]{1,0:T(8,128)S(1)} %get-tuple-element.19.along_ref, f32[128,128]{1,0:T(8,128)S(1)} %get-tuple-element.17.gram_time_ref), custom_call_target="tpu_custom_call" | custom-call | tf_op jit(solution)/shard_map/third_product/pallas_call | solution.py:239
  90.8 14.0 %all_to_all.40.in_ref = f32[16,24,128]{2,1,0:T(8,128)S(1)} all-to-all(f32[16,24,128]{2,1,0:T(8,128)S(1)} %get-tuple-element.20), channel_id=1, replica_groups=mesh['gx'=16,'gy'=16] {'gy'}, dimensions={0} | all-to-all | bytes 393216 | tf_op jit(solution)/shard_map/all_to_all | solution.py:252
  104.9 11.6 %all_to_all.41.in_ref = f32[16,24,128]{2,1,0:T(8,128)S(1)} all-to-all(f32[16,24,128]{2,1,0:T(8,128)S(1)} %sum_c.1), channel_id=1, replica_groups=mesh['gx'=16,'gy'=16] {'gx'}, dimensions={0} | all-to-all | bytes 393216 | tf_op jit(solution)/shard_map/all_to_all | solution.py:252
  116.4 4.5 %finish.1 = (f32[24,128]{1,0:T(8,128)}, f32[24,128]{1,0:T(8,128)}, f32[16,128]{1,0:T(8,128)}) custom-call(f32[16,24,128]{2,1,0:T(8,128)S(1)} %all_to_all.41.in_ref, f32[128,128]{1,0:T(8,128)S(1)} %get-tuple-element.21.gram_a_ref, f32[1,128]{1,0:T(1,128)S(1)} %get-tuple-element.22.norm_a_ref, f32[24,128]{1,0:T(8,128)S(1)} %get-tuple-element.23.raw_a_ref, ...), custom_call_target="tpu_custom_call" | custom-call | tf_op jit(solution)/shard_map/finish/pallas_call | solution.py:239
  (4 shorter events, 0.1 us)
Async XLA Ops:
  0.6 14.4 %copy-start.1 = (f32[16,128]{1,0:T(8,128)S(1)}, f32[16,128]{1,0:T(8,128)}, u32[]{:S(2)}) copy-start(f32[16,128]{1,0:T(8,128)} %time_ref.3) | copy-start | bytes 24580
  0.6 0.7 copy-start.2
  1.4 13.7 %copy-start = (f32[16,384,384]{2,1,0:T(8,128)S(1)}, f32[16,384,384]{2,1,0:T(8,128)}, u32[]{:S(2)}) copy-start(f32[16,384,384]{2,1,0:T(8,128)} %tensor_ref.1) | copy-start | bytes 28311556

commit v5 on v4

--- a/solution.py
+++ b/solution.py
@@ -13,7 +13,7 @@
 bf16 = jnp.bfloat16
 VMEM = pltpu.VMEM
 TILE = 8
-PAIR = 2
+PAIR = 8
 LOOK = 2
 
 
@@ -81,10 +81,11 @@
             jnp.concatenate([part.astype(f32) if v == block else zero for v in range(blocks)], axis=0).astype(bf16)
             for part in three_parts(result)
         ]
-        pair = jnp.concatenate([r_high, r_middle], axis=1)
-        large = raw_dot(jnp.concatenate([c_high, c_middle], axis=1), jnp.concatenate([pair, pair], axis=0), 1, 0)
-        small = raw_dot(jnp.concatenate([c_high, c_low], axis=1), jnp.concatenate([r_low, r_high], axis=0), 1, 0)
-        product = large[:, :n] + (large[:, n:] + small)
+        none = jnp.zeros_like(r_high)
+        right = [(r_high, r_middle), (r_high, r_middle), (r_low, none), (r_high, none)]
+        right = jnp.concatenate([jnp.concatenate(pair, axis=1) for pair in right], axis=0)
+        product = raw_dot(jnp.concatenate([c_high, c_middle, c_high, c_low], axis=1), right, 1, 0)
+        product = product[:, :n] + product[:, n:]
         near = [(block + 1 + q) % blocks for q in range(LOOK)]
         update = []
         for v in range(blocks):

time: 121 us -> 121 us (level)
  no operation moved by 1% of the time
where the time goes in v5:
time: 121 us; the launch traced here: 120 us
  blocking collectives  100 us (83%)
  Pallas kernels  18.8 us (16%)
    all_to_all x7, blocking collectives, exchange(): return lax.all_to_all(value, axis, 0, 0)  100 us
    pallas_call x8, Pallas kernels, call(): pl.pallas_call(kernel, out_shape=shapes[0] if single else shapes, in_spec...  18.8 us

profile of v5, /device:TPU:1, one launch (start us, length us, event | category | flops | bytes accessed | tf_op | source)
XLA Modules:
  0.0 120.4 jit_solution(17709786759037898066)
XLA Ops:
  0.6 0.0 copy-start.1
  0.6 0.0 copy-start.2
  0.7 0.7 copy-done.2
  1.4 0.0 copy-start
  1.4 13.7 %all_to_all.35.factor_ref = f32[16,24,128]{2,1,0:T(8,128)S(1)} all-to-all(f32[16,24,128]{2,1,0:T(8,128)S(1)} %spread.1), channel_id=1, replica_groups=mesh['gx'=16,'gy'=16] {'gx'}, dimensions={0} | all-to-all | bytes 393216 | tf_op jit(solution)/shard_map/all_to_all | solution.py:253
  15.0 0.0 copy-done.1
  15.0 0.0 copy-done
  15.1 3.1 %first_product.1 = (f32[16,32,128]{2,1,0:T(8,128)S(1)}, bf16[384,6144]{1,0:T(8,128)(2,1)S(1)}, bf16[384,6144]{1,0:T(8,128)(2,1)S(1)}, f32[128,128]{1,0:T(8,128)S(1)}) custom-call(f32[16,384,384]{2,1,0:T(8,128)S(1)} %copy-done, f32[16,24,128]{2,1,0:T(8,128)S(1)} %all_to_all.35.factor_ref, f32[16,128]{1,0:T(8,128)S(1)} %copy-done.1), custom_call_target="tpu_custom_call" | custom-call | tf_op jit(solution)/shard_map/first_product/pallas_call | solution.py:240
  18.1 22.9 %all_to_all.36.in_ref = f32[16,32,128]{2,1,0:T(8,128)S(1)} all-to-all(f32[16,32,128]{2,1,0:T(8,128)S(1)} %get-tuple-element.16), channel_id=1, replica_groups=mesh['gx'=16,'gy'=16] {'gy'}, dimensions={0} | all-to-all | bytes 524288 | tf_op jit(solution)/shard_map/all_to_all | solution.py:253
  41.0 14.8 %all_to_all.37.in_ref = f32[16,32,128]{2,1,0:T(8,128)S(1)} all-to-all(f32[16,32,128]{2,1,0:T(8,128)S(1)} %sum_a.1), channel_id=1, replica_groups=mesh['gx'=16,'gy'=16] {'gy'}, dimensions={0} | all-to-all | bytes 524288 | tf_op jit(solution)/shard_map/all_to_all | solution.py:253
  55.8 6.9 %second_product.1 = (f32[16,32,128]{2,1,0:T(8,128)S(1)}, f32[128,6144]{1,0:T(8,128)S(1)}, f32[24,128]{1,0:T(8,128)S(1)}) custom-call(bf16[384,6144]{1,0:T(8,128)(2,1)S(1)} %get-tuple-element.14.high_ref, bf16[384,6144]{1,0:T(8,128)(2,1)S(1)} %get-tuple-element.15.low_ref, f32[16,32,128]{2,1,0:T(8,128)S(1)} %all_to_all.37.in_ref, f32[16,128]{1,0:T(8,128)S(1)} %copy-done.1, ...), custom_call_target="tpu_custom_call" | custom-call | tf_op jit(solution)/shard_map/second_product/pallas_call | solution.py:240
  62.7 13.0 %all_to_all.38.in_ref = f32[16,32,128]{2,1,0:T(8,128)S(1)} all-to-all(f32[16,32,128]{2,1,0:T(8,128)S(1)} %get-tuple-element.18), channel_id=1, replica_groups=mesh['gx'=16,'gy'=16] {'gx'}, dimensions={0} | all-to-all | bytes 524288 | tf_op jit(solution)/shard_map/all_to_all | solution.py:253
  75.8 10.3 %all_to_all.39.in_ref = f32[16,32,128]{2,1,0:T(8,128)S(1)} all-to-all(f32[16,32,128]{2,1,0:T(8,128)S(1)} %sum_b.1), channel_id=1, replica_groups=mesh['gx'=16,'gy'=16] {'gx'}, dimensions={0} | all-to-all | bytes 524288 | tf_op jit(solution)/shard_map/all_to_all | solution.py:253
  86.1 4.4 %third_product.1 = (f32[16,24,128]{2,1,0:T(8,128)S(1)}, f32[24,128]{1,0:T(8,128)S(1)}, f32[128,128]{1,0:T(8,128)S(1)}, f32[1,128]{1,0:T(1,128)S(1)}) custom-call(f32[16,32,128]{2,1,0:T(8,128)S(1)} %all_to_all.39.in_ref, f32[128,6144]{1,0:T(8,128)S(1)} %get-tuple-element.19.along_ref, f32[128,128]{1,0:T(8,128)S(1)} %get-tuple-element.17.gram_time_ref), custom_call_target="tpu_custom_call" | custom-call | tf_op jit(solution)/shard_map/third_product/pallas_call | solution.py:240
  90.4 14.0 %all_to_all.40.in_ref = f32[16,24,128]{2,1,0:T(8,128)S(1)} all-to-all(f32[16,24,128]{2,1,0:T(8,128)S(1)} %get-tuple-element.20), channel_id=1, replica_groups=mesh['gx'=16,'gy'=16] {'gy'}, dimensions={0} | all-to-all | bytes 393216 | tf_op jit(solution)/shard_map/all_to_all | solution.py:253
  104.5 11.6 %all_to_all.41.in_ref = f32[16,24,128]{2,1,0:T(8,128)S(1)} all-to-all(f32[16,24,128]{2,1,0:T(8,128)S(1)} %sum_c.1), channel_id=1, replica_groups=mesh['gx'=16,'gy'=16] {'gx'}, dimensions={0} | all-to-all | bytes 393216 | tf_op jit(solution)/shard_map/all_to_all | solution.py:253
  116.0 4.4 %finish.1 = (f32[24,128]{1,0:T(8,128)}, f32[24,128]{1,0:T(8,128)}, f32[16,128]{1,0:T(8,128)}) custom-call(f32[16,24,128]{2,1,0:T(8,128)S(1)} %all_to_all.41.in_ref, f32[128,128]{1,0:T(8,128)S(1)} %get-tuple-element.21.gram_a_ref, f32[1,128]{1,0:T(1,128)S(1)} %get-tuple-element.22.norm_a_ref, f32[24,128]{1,0:T(8,128)S(1)} %get-tuple-element.23.raw_a_ref, ...), custom_call_target="tpu_custom_call" | custom-call | tf_op jit(solution)/shard_map/finish/pallas_call | solution.py:240
  (4 shorter events, 0.1 us)
Async XLA Ops:
  0.6 14.4 %copy-start.1 = (f32[16,128]{1,0:T(8,128)S(1)}, f32[16,128]{1,0:T(8,128)}, u32[]{:S(2)}) copy-start(f32[16,128]{1,0:T(8,128)} %time_ref.3) | copy-start | bytes 24580
  0.6 0.7 copy-start.2
  1.4 13.7 %copy-start = (f32[16,384,384]{2,1,0:T(8,128)S(1)}, f32[16,384,384]{2,1,0:T(8,128)}, u32[]{:S(2)}) copy-start(f32[16,384,384]{2,1,0:T(8,128)} %tensor_ref.1) | copy-start | bytes 28311556

commit v6 on v5

--- a/solution.py
+++ b/solution.py
@@ -166,13 +166,14 @@
         out_ref[d] = total
 
 
-def second_product(high_ref, low_ref, in_ref, time_ref, gram_time_ref, out_ref, along_ref, raw_ref):
+def second_product(high_ref, low_ref, in_ref, time_ref, gram_time_ref, out_ref, along_ref, own_ref, inverse_ref):
     snapshots, rank = time_ref.shape
     rows = in_ref.shape[1] - rank // in_ref.shape[0]
     gram_old, gram_time = unpack(in_ref, rows, in_ref.shape[1] - rows), gram_time_ref[...]
     inverse = metric_inverse(gram_old, gram_time, diagonal(gram_old), diagonal(gram_time))
     turned = dot(inverse, unpack(in_ref, 0, rows), 1, 1)
-    raw_ref[...] = dot(in_ref[lax.axis_index("gy"), :rows, :], inverse, 1, 1)
+    own_ref[...] = in_ref[lax.axis_index("gy"), :rows, :]
+    inverse_ref[...] = inverse
     gram = dot(turned, turned, 1, 1)
     high, low = split(turned)
     both = jnp.concatenate([high, low], axis=0)
@@ -190,7 +191,7 @@
     pack(out_ref, total.T, gram)
 
 
-def third_product(in_ref, along_ref, gram_time_ref, out_ref, raw_ref, gram_ref, norm_ref):
+def third_product(in_ref, along_ref, gram_time_ref, out_ref, own_ref, inverse_ref, gram_ref, norm_ref):
     rank = gram_time_ref.shape[0]
     extra = rank // in_ref.shape[0]
     rows = in_ref.shape[1] - extra
@@ -199,7 +200,8 @@
     gram_time = gram_time_ref[...]
     inverse = metric_inverse(gram_a, gram_time, ends, diagonal(gram_time))
     turned = dot(inverse, unpack(in_ref, 0, rows) / norm_row, 1, 1)
-    raw_ref[...] = dot(in_ref[lax.axis_index("gx"), :rows, :] / norm_row, inverse, 1, 1)
+    own_ref[...] = in_ref[lax.axis_index("gx"), :rows, :] / norm_row
+    inverse_ref[...] = inverse
     gram_ref[...] = gram_a
     norm_ref[...] = norm_row
     gram = dot(turned, turned, 1, 1)
@@ -223,14 +225,16 @@
     return value
 
 
-def finish(size_a, size_b, in_ref, gram_a_ref, norm_a_ref, raw_a_ref, raw_b_ref, factor_a_ref, factor_b_ref, time_ref):
+def finish(size_a, size_b, in_ref, gram_a_ref, norm_a_ref, own_a_ref, inverse_a_ref, own_b_ref, inverse_b_ref, factor_a_ref, factor_b_ref, time_ref):
     snapshots = time_ref.shape[0]
     norm_row, _, gram_b, ends = scaled(unpack(in_ref, snapshots, in_ref.shape[1] - snapshots))
     gram_a = gram_a_ref[...]
     products = jnp.sum(in_ref[:, :snapshots, :], axis=0) / norm_row
+    raw_a = dot(own_a_ref[...], inverse_a_ref[...], 1, 1)
+    raw_b = dot(own_b_ref[...], inverse_b_ref[...], 1, 1)
+    factor_a_ref[...] = raw_a / norm_a_ref[...] * jnp.sqrt(f32(size_a))
+    factor_b_ref[...] = raw_b / norm_row * jnp.sqrt(f32(size_b))
     time_ref[...] = dot(products, metric_inverse(gram_b, gram_a, ends, diagonal(gram_a)), 1, 0)
-    factor_a_ref[...] = raw_a_ref[...] / norm_a_ref[...] * jnp.sqrt(f32(size_a))
-    factor_b_ref[...] = raw_b_ref[...] / norm_row * jnp.sqrt(f32(size_b))
 
 
 def call(kernel, inputs, outputs, name, spaces=None, scratch=(), limit=16 << 20, cost=None):
@@ -273,19 +277,19 @@
     sent = exchange(sent, "gy")
     sent = call(sum_and_copy, (sent,), [sent.shape], "sum_a")
     sent = exchange(sent, "gy")
-    sent, along, raw_a = call(
+    sent, along, own_a, inverse_a = call(
         second_product,
         (high, low, sent, time_init, gram_time),
-        [(nx, own_j + extra_x, rank), (rank, snapshots * rows_j), (own_i, rank)],
+        [(nx, own_j + extra_x, rank), (rank, snapshots * rows_j), (own_i, rank), (rank, rank)],
         "second_product",
     )
     sent = exchange(sent, "gx")
     sent = call(sum_and_copy, (sent,), [sent.shape], "sum_b")
     sent = exchange(sent, "gx")
-    sent, raw_b, gram_a, norm_a = call(
+    sent, own_b, inverse_b, gram_a, norm_a = call(
         third_product,
         (sent, along, gram_time),
-        [(ny, snapshots + extra_x, rank), (own_j, rank), (rank, rank), (1, rank)],
+        [(ny, snapshots + extra_x, rank), (own_j, rank), (rank, rank), (rank, rank), (1, rank)],
         "third_product",
     )
     sent = exchange(sent, "gy")
@@ -293,7 +297,7 @@
     sent = exchange(sent, "gx")
     return call(
         functools.partial(finish, rows_i * nx, rows_j * ny),
-        (sent, gram_a, norm_a, raw_a, raw_b),
+        (sent, gram_a, norm_a, own_a, inverse_a, own_b, inverse_b),
         [(own_i, rank), (own_j, rank), (snapshots, rank)],
         "finish",
     )

time: 121 us -> 121 us (level)
  no operation moved by 1% of the time
where the time goes in v6:
time: 121 us; the launch traced here: 120 us
  blocking collectives  100 us (83%)
  Pallas kernels  18.6 us (15%)
    all_to_all x7, blocking collectives, exchange(): return lax.all_to_all(value, axis, 0, 0)  100 us
    pallas_call x8, Pallas kernels, call(): pl.pallas_call(kernel, out_shape=shapes[0] if single else shapes, in_spec...  18.6 us

profile of v6, /device:TPU:1, one launch (start us, length us, event | category | flops | bytes accessed | tf_op | source)
XLA Modules:
  0.0 120.2 jit_solution(8974826572306174777)
XLA Ops:
  0.6 0.0 copy-start.1
  0.6 0.0 copy-start.2
  0.7 0.7 copy-done.2
  1.4 0.0 copy-start
  1.4 13.7 %all_to_all.35.factor_ref = f32[16,24,128]{2,1,0:T(8,128)S(1)} all-to-all(f32[16,24,128]{2,1,0:T(8,128)S(1)} %spread.1), channel_id=1, replica_groups=mesh['gx'=16,'gy'=16] {'gx'}, dimensions={0} | all-to-all | bytes 393216 | tf_op jit(solution)/shard_map/all_to_all | solution.py:257
  15.0 0.0 copy-done.1
  15.0 0.0 copy-done
  15.1 3.1 %first_product.1 = (f32[16,32,128]{2,1,0:T(8,128)S(1)}, bf16[384,6144]{1,0:T(8,128)(2,1)S(1)}, bf16[384,6144]{1,0:T(8,128)(2,1)S(1)}, f32[128,128]{1,0:T(8,128)S(1)}) custom-call(f32[16,384,384]{2,1,0:T(8,128)S(1)} %copy-done, f32[16,24,128]{2,1,0:T(8,128)S(1)} %all_to_all.35.factor_ref, f32[16,128]{1,0:T(8,128)S(1)} %copy-done.1), custom_call_target="tpu_custom_call" | custom-call | tf_op jit(solution)/shard_map/first_product/pallas_call | solution.py:244
  18.1 22.9 %all_to_all.36.in_ref = f32[16,32,128]{2,1,0:T(8,128)S(1)} all-to-all(f32[16,32,128]{2,1,0:T(8,128)S(1)} %get-tuple-element.18), channel_id=1, replica_groups=mesh['gx'=16,'gy'=16] {'gy'}, dimensions={0} | all-to-all | bytes 524288 | tf_op jit(solution)/shard_map/all_to_all | solution.py:257
  41.0 14.8 %all_to_all.37.in_ref = f32[16,32,128]{2,1,0:T(8,128)S(1)} all-to-all(f32[16,32,128]{2,1,0:T(8,128)S(1)} %sum_a.1), channel_id=1, replica_groups=mesh['gx'=16,'gy'=16] {'gy'}, dimensions={0} | all-to-all | bytes 524288 | tf_op jit(solution)/shard_map/all_to_all | solution.py:257
  55.8 6.8 %second_product.1 = (f32[16,32,128]{2,1,0:T(8,128)S(1)}, f32[128,6144]{1,0:T(8,128)S(1)}, f32[24,128]{1,0:T(8,128)S(1)}, f32[128,128]{1,0:T(8,128)S(1)}) custom-call(bf16[384,6144]{1,0:T(8,128)(2,1)S(1)} %get-tuple-element.16.high_ref, bf16[384,6144]{1,0:T(8,128)(2,1)S(1)} %get-tuple-element.17.low_ref, f32[16,32,128]{2,1,0:T(8,128)S(1)} %all_to_all.37.in_ref, ...), custom_call_target="tpu_custom_call" | custom-call | tf_op jit(solution)/shard_map/second_product/pallas_call | solution.py:244
  62.6 13.0 %all_to_all.38.in_ref = f32[16,32,128]{2,1,0:T(8,128)S(1)} all-to-all(f32[16,32,128]{2,1,0:T(8,128)S(1)} %get-tuple-element.20), channel_id=1, replica_groups=mesh['gx'=16,'gy'=16] {'gx'}, dimensions={0} | all-to-all | bytes 524288 | tf_op jit(solution)/shard_map/all_to_all | solution.py:257
  75.7 10.3 %all_to_all.39.in_ref = f32[16,32,128]{2,1,0:T(8,128)S(1)} all-to-all(f32[16,32,128]{2,1,0:T(8,128)S(1)} %sum_b.1), channel_id=1, replica_groups=mesh['gx'=16,'gy'=16] {'gx'}, dimensions={0} | all-to-all | bytes 524288 | tf_op jit(solution)/shard_map/all_to_all | solution.py:257
  86.0 4.3 %third_product.1 = (f32[16,24,128]{2,1,0:T(8,128)S(1)}, f32[24,128]{1,0:T(8,128)S(1)}, f32[128,128]{1,0:T(8,128)S(1)}, f32[128,128]{1,0:T(8,128)S(1)}, f32[1,128]{1,0:T(1,128)S(1)}) custom-call(f32[16,32,128]{2,1,0:T(8,128)S(1)} %all_to_all.39.in_ref, f32[128,6144]{1,0:T(8,128)S(1)} %get-tuple-element.21.along_ref, ...), custom_call_target="tpu_custom_call" | custom-call | tf_op jit(solution)/shard_map/third_product/pallas_call | solution.py:244
  90.3 14.0 %all_to_all.40.in_ref = f32[16,24,128]{2,1,0:T(8,128)S(1)} all-to-all(f32[16,24,128]{2,1,0:T(8,128)S(1)} %get-tuple-element.22), channel_id=1, replica_groups=mesh['gx'=16,'gy'=16] {'gy'}, dimensions={0} | all-to-all | bytes 393216 | tf_op jit(solution)/shard_map/all_to_all | solution.py:257
  104.3 11.6 %all_to_all.41.in_ref = f32[16,24,128]{2,1,0:T(8,128)S(1)} all-to-all(f32[16,24,128]{2,1,0:T(8,128)S(1)} %sum_c.1), channel_id=1, replica_groups=mesh['gx'=16,'gy'=16] {'gx'}, dimensions={0} | all-to-all | bytes 393216 | tf_op jit(solution)/shard_map/all_to_all | solution.py:257
  115.9 4.3 %finish.1 = (f32[24,128]{1,0:T(8,128)}, f32[24,128]{1,0:T(8,128)}, f32[16,128]{1,0:T(8,128)}) custom-call(f32[16,24,128]{2,1,0:T(8,128)S(1)} %all_to_all.41.in_ref, f32[128,128]{1,0:T(8,128)S(1)} %get-tuple-element.23.gram_a_ref, f32[1,128]{1,0:T(1,128)S(1)} %get-tuple-element.24.norm_a_ref, f32[24,128]{1,0:T(8,128)S(1)} %get-tuple-element.25.own_a_ref, ...), custom_call_target="tpu_custom_call" | custom-call | tf_op jit(solution)/shard_map/finish/pallas_call | solution.py:244
  (4 shorter events, 0.1 us)
Async XLA Ops:
  0.6 14.4 %copy-start.1 = (f32[16,128]{1,0:T(8,128)S(1)}, f32[16,128]{1,0:T(8,128)}, u32[]{:S(2)}) copy-start(f32[16,128]{1,0:T(8,128)} %time_ref.3) | copy-start | bytes 24580
  0.6 0.7 copy-start.2
  1.4 13.7 %copy-start = (f32[16,384,384]{2,1,0:T(8,128)S(1)}, f32[16,384,384]{2,1,0:T(8,128)}, u32[]{:S(2)}) copy-start(f32[16,384,384]{2,1,0:T(8,128)} %tensor_ref.1) | copy-start | bytes 28311556

commit v7 on v5

--- a/solution.py
+++ b/solution.py
@@ -121,7 +121,7 @@
     across, down = diagonal(gram_raw)
     norm_row, norm_column = jnp.sqrt(across + epsilon), jnp.sqrt(down + epsilon)
     ends = across / (norm_row * norm_row), down / (norm_column * norm_column)
-    return norm_row, norm_column, gram_raw / (norm_column * norm_row), ends
+    return norm_row, norm_column, gram_raw * ((1.0 / norm_column) * (1.0 / norm_row)), ends
 
 
 def unpack(ref, at, size):
@@ -198,8 +198,8 @@
     norm_row, norm_column, gram_a, ends = scaled(unpack(in_ref, rows, extra))
     gram_time = gram_time_ref[...]
     inverse = metric_inverse(gram_a, gram_time, ends, diagonal(gram_time))
-    turned = dot(inverse, unpack(in_ref, 0, rows) / norm_row, 1, 1)
-    raw_ref[...] = dot(in_ref[lax.axis_index("gx"), :rows, :] / norm_row, inverse, 1, 1)
+    turned = dot(inverse, unpack(in_ref, 0, rows) * (1.0 / norm_row), 1, 1)
+    raw_ref[...] = dot(in_ref[lax.axis_index("gx"), :rows, :] * (1.0 / norm_row), inverse, 1, 1)
     gram_ref[...] = gram_a
     norm_ref[...] = norm_row
     gram = dot(turned, turned, 1, 1)

time: 121 us -> 121 us (level)
  no operation moved by 1% of the time
where the time goes in v7:
time: 121 us; the launch traced here: 120 us
  blocking collectives  100 us (83%)
  Pallas kernels  18.8 us (16%)
    all_to_all x7, blocking collectives, exchange(): return lax.all_to_all(value, axis, 0, 0)  100 us
    pallas_call x8, Pallas kernels, call(): pl.pallas_call(kernel, out_shape=shapes[0] if single else shapes, in_spec...  18.8 us

profile of v7, /device:TPU:1, one launch (start us, length us, event | category | flops | bytes accessed | tf_op | source)
XLA Modules:
  0.0 120.4 jit_solution(2365064441286278397)
XLA Ops:
  0.6 0.0 copy-start.1
  0.6 0.0 copy-start.2
  0.7 0.7 copy-done.2
  1.4 0.0 copy-start
  1.4 13.7 %all_to_all.35.factor_ref = f32[16,24,128]{2,1,0:T(8,128)S(1)} all-to-all(f32[16,24,128]{2,1,0:T(8,128)S(1)} %spread.1), channel_id=1, replica_groups=mesh['gx'=16,'gy'=16] {'gx'}, dimensions={0} | all-to-all | bytes 393216 | tf_op jit(solution)/shard_map/all_to_all | solution.py:253
  15.0 0.0 copy-done.1
  15.0 0.0 copy-done
  15.1 3.1 %first_product.1 = (f32[16,32,128]{2,1,0:T(8,128)S(1)}, bf16[384,6144]{1,0:T(8,128)(2,1)S(1)}, bf16[384,6144]{1,0:T(8,128)(2,1)S(1)}, f32[128,128]{1,0:T(8,128)S(1)}) custom-call(f32[16,384,384]{2,1,0:T(8,128)S(1)} %copy-done, f32[16,24,128]{2,1,0:T(8,128)S(1)} %all_to_all.35.factor_ref, f32[16,128]{1,0:T(8,128)S(1)} %copy-done.1), custom_call_target="tpu_custom_call" | custom-call | tf_op jit(solution)/shard_map/first_product/pallas_call | solution.py:240
  18.1 22.9 %all_to_all.36.in_ref = f32[16,32,128]{2,1,0:T(8,128)S(1)} all-to-all(f32[16,32,128]{2,1,0:T(8,128)S(1)} %get-tuple-element.16), channel_id=1, replica_groups=mesh['gx'=16,'gy'=16] {'gy'}, dimensions={0} | all-to-all | bytes 524288 | tf_op jit(solution)/shard_map/all_to_all | solution.py:253
  41.0 14.8 %all_to_all.37.in_ref = f32[16,32,128]{2,1,0:T(8,128)S(1)} all-to-all(f32[16,32,128]{2,1,0:T(8,128)S(1)} %sum_a.1), channel_id=1, replica_groups=mesh['gx'=16,'gy'=16] {'gy'}, dimensions={0} | all-to-all | bytes 524288 | tf_op jit(solution)/shard_map/all_to_all | solution.py:253
  55.8 6.9 %second_product.1 = (f32[16,32,128]{2,1,0:T(8,128)S(1)}, f32[128,6144]{1,0:T(8,128)S(1)}, f32[24,128]{1,0:T(8,128)S(1)}) custom-call(bf16[384,6144]{1,0:T(8,128)(2,1)S(1)} %get-tuple-element.14.high_ref, bf16[384,6144]{1,0:T(8,128)(2,1)S(1)} %get-tuple-element.15.low_ref, f32[16,32,128]{2,1,0:T(8,128)S(1)} %all_to_all.37.in_ref, f32[16,128]{1,0:T(8,128)S(1)} %copy-done.1, ...), custom_call_target="tpu_custom_call" | custom-call | tf_op jit(solution)/shard_map/second_product/pallas_call | solution.py:240
  62.7 13.0 %all_to_all.38.in_ref = f32[16,32,128]{2,1,0:T(8,128)S(1)} all-to-all(f32[16,32,128]{2,1,0:T(8,128)S(1)} %get-tuple-element.18), channel_id=1, replica_groups=mesh['gx'=16,'gy'=16] {'gx'}, dimensions={0} | all-to-all | bytes 524288 | tf_op jit(solution)/shard_map/all_to_all | solution.py:253
  75.8 10.3 %all_to_all.39.in_ref = f32[16,32,128]{2,1,0:T(8,128)S(1)} all-to-all(f32[16,32,128]{2,1,0:T(8,128)S(1)} %sum_b.1), channel_id=1, replica_groups=mesh['gx'=16,'gy'=16] {'gx'}, dimensions={0} | all-to-all | bytes 524288 | tf_op jit(solution)/shard_map/all_to_all | solution.py:253
  86.1 4.4 %third_product.1 = (f32[16,24,128]{2,1,0:T(8,128)S(1)}, f32[24,128]{1,0:T(8,128)S(1)}, f32[128,128]{1,0:T(8,128)S(1)}, f32[1,128]{1,0:T(1,128)S(1)}) custom-call(f32[16,32,128]{2,1,0:T(8,128)S(1)} %all_to_all.39.in_ref, f32[128,6144]{1,0:T(8,128)S(1)} %get-tuple-element.19.along_ref, f32[128,128]{1,0:T(8,128)S(1)} %get-tuple-element.17.gram_time_ref), custom_call_target="tpu_custom_call" | custom-call | tf_op jit(solution)/shard_map/third_product/pallas_call | solution.py:240
  90.4 14.0 %all_to_all.40.in_ref = f32[16,24,128]{2,1,0:T(8,128)S(1)} all-to-all(f32[16,24,128]{2,1,0:T(8,128)S(1)} %get-tuple-element.20), channel_id=1, replica_groups=mesh['gx'=16,'gy'=16] {'gy'}, dimensions={0} | all-to-all | bytes 393216 | tf_op jit(solution)/shard_map/all_to_all | solution.py:253
  104.5 11.6 %all_to_all.41.in_ref = f32[16,24,128]{2,1,0:T(8,128)S(1)} all-to-all(f32[16,24,128]{2,1,0:T(8,128)S(1)} %sum_c.1), channel_id=1, replica_groups=mesh['gx'=16,'gy'=16] {'gx'}, dimensions={0} | all-to-all | bytes 393216 | tf_op jit(solution)/shard_map/all_to_all | solution.py:253
  116.0 4.4 %finish.1 = (f32[24,128]{1,0:T(8,128)}, f32[24,128]{1,0:T(8,128)}, f32[16,128]{1,0:T(8,128)}) custom-call(f32[16,24,128]{2,1,0:T(8,128)S(1)} %all_to_all.41.in_ref, f32[128,128]{1,0:T(8,128)S(1)} %get-tuple-element.21.gram_a_ref, f32[1,128]{1,0:T(1,128)S(1)} %get-tuple-element.22.norm_a_ref, f32[24,128]{1,0:T(8,128)S(1)} %get-tuple-element.23.raw_a_ref, ...), custom_call_target="tpu_custom_call" | custom-call | tf_op jit(solution)/shard_map/finish/pallas_call | solution.py:240
  (4 shorter events, 0.1 us)
Async XLA Ops:
  0.6 14.4 %copy-start.1 = (f32[16,128]{1,0:T(8,128)S(1)}, f32[16,128]{1,0:T(8,128)}, u32[]{:S(2)}) copy-start(f32[16,128]{1,0:T(8,128)} %time_ref.3) | copy-start | bytes 24580
  0.6 0.7 copy-start.2
  1.4 13.7 %copy-start = (f32[16,384,384]{2,1,0:T(8,128)S(1)}, f32[16,384,384]{2,1,0:T(8,128)}, u32[]{:S(2)}) copy-start(f32[16,384,384]{2,1,0:T(8,128)} %tensor_ref.1) | copy-start | bytes 28311556
